TPU v7x, 32 devices: a whole 2x2x4 slice. The times are simulated.
32 devices in a mesh: parts: 2 (over y), tensor: 4 (over z), dp: 4 (over x, core).
Axes of the slice: x: 2, y: 2, z: 4, core: 2. Of those that a mesh axis runs over, the one named last changes fastest.
Arguments:
- inputs: bfloat16 [4096, 8192], P(('parts', 'dp'), 'tensor'), parts along dimension 0, may hold values from -6 to 6
- out_grad: bfloat16 [4096, 4, 2048], P(('parts', 'dp'), None, 'tensor'), parts along dimension 0, may hold values from -6 to 6
- gate_pre: bfloat16 [4096, 28672], P(('parts', 'dp'), 'tensor'), parts along dimension 0, may hold values from -8 to 8
- down_weight: bfloat16 [28672, 8192], P('tensor', 'dp'), may hold values from -0.03125 to 0.03125
- proj_in: bfloat16 [8192, 64], P('tensor'), may hold values from -0.0625 to 0.0625
- proj_out: bfloat16 [28672, 64], P('tensor'), may hold values from -0.09375 to 0.09375
- queries: bfloat16 [256, 4096], P('tensor', 'dp'), may hold values from -0.1875 to 0.1875
Outputs:
- scores: float32 [256, 4096], P('tensor', ('parts', 'dp')), parts along dimension 1
There are 2 independent parts, one for each index of `parts`. A program takes and returns all parts, laid end to end along the dimension named above; an argument that names none is the same for every part. Nothing has to cross between parts.
All inputs are finite; a program needn't handle non-finite values.
Results may differ from a plain program's by a relative error of at most 0.0041.
Values may be sent and summed in bfloat16 or wider, within the bound.
No kernel may reach another device: no remote copies, remote signals or barrier semaphores. Data moves between devices by JAX's collectives and lax.ppermute only.
A program may use at most 320 MiB of HBM per device.

v0:
```python
import jax
import jax.numpy as jnp
from jax import lax
from jax.sharding import PartitionSpec as P


def contract_last(left, right):
    return lax.dot_general(
        left, right, (((1,), (1,)), ((), ())), preferred_element_type=jnp.float32
    )


def on_device(inputs, out_grad, gate_pre, down_weight, proj_in, proj_out, queries):
    row_count = out_grad.shape[0]
    input_proj = lax.psum(jnp.dot(inputs, proj_in, preferred_element_type=jnp.float32), "tensor")
    gathered = lax.all_gather(out_grad, "tensor", axis=2, tiled=True)
    full_grad = gathered.reshape(row_count, -1)
    columns = full_grad
    hidden_grad = contract_last(columns, lax.all_gather(down_weight, "dp", axis=1, tiled=True))
    up_grad = (hidden_grad * jax.nn.silu(gate_pre.astype(jnp.float32))).astype(jnp.bfloat16)
    grad_part = jnp.dot(up_grad, proj_out, preferred_element_type=jnp.float32)
    grad_proj = lax.psum(grad_part, "tensor")
    features = (
        (input_proj[:, :, None] * grad_proj[:, None, :])
        .reshape(input_proj.shape[0], -1)
        .astype(jnp.bfloat16)
    )
    columns = features
    return contract_last(lax.all_gather(queries, "dp", axis=1, tiled=True), columns)


def solution(mesh):
    return jax.shard_map(
        on_device,
        mesh=mesh,
        in_specs=(
            P(("parts", "dp"), "tensor"),
            P(("parts", "dp"), None, "tensor"),
            P(("parts", "dp"), "tensor"),
            P("tensor", "dp"),
            P("tensor", None),
            P("tensor", None),
            P("tensor", "dp"),
        ),
        out_specs=P("tensor", ("parts", "dp")),
        check_vma=False,
    )
```

profile of v0, /device:TPU:0, one launch (start us, length us, event | category | flops | bytes accessed | tf_op | source)
XLA Modules:
  0.0 961.4 jit_solution(3376615055738195482)
XLA Ops:
  6.5 0.0 copy-start
  6.5 0.0 all-gather.3.cloned.1.call-start
  6.5 0.7 all-gather.3.cloned.1.call-update
  7.3 0.0 copy-start.2
  7.3 0.0 all-gather.5.cloned.1.call-start
  7.3 0.7 all-gather.5.cloned.1.call-update
  8.0 0.0 all-reduce.3.cloned.1.call-start
  8.1 0.1 copy-done
  8.1 0.2 copy-done.2
  8.4 1.4 fusion.8
  9.8 151.0 %all-gather.3.cloned.1.call-done = bf16[512,4,2048]{2,1,0:T(4,128)(2,1)} async-done(((bf16[512,4,512]{2,1,0:T(4,128)(2,1)}), bf16[512,4,2048]{2,1,0:T(4,128)(2,1)}) %all-gather.3.cloned.1.call-update) | async-done | bytes 8388624 | tf_op jit(solution)/shard_map/all_gather | solution.py:16
  160.8 19.3 %copy.10 = bf16[64,8,4,2048]{3,1,2,0:T(8,128)(2,1)} copy(bf16[64,8,4,2048]{3,2,1,0:T(4,128)(2,1)} %bitcast.21) | data formatting | bytes 16777216
  180.1 660.0 %all-gather.5.cloned.1.call-done = bf16[7168,8192]{1,0:T(8,128)(2,1)} async-done(((bf16[7168,2048]{1,0:T(8,128)(2,1)}), bf16[7168,8192]{1,0:T(8,128)(2,1)}) %all-gather.5.cloned.1.call-update) | async-done | bytes 117440528 | tf_op jit(solution)/shard_map/all_gather | solution.py:19
  840.1 0.0 copy-start.1
  840.1 70.9 %fusion.4.clone.4 = bf16[512,7168]{1,0:T(8,128)(2,1)S(1)} fusion(bf16[512,7168]{1,0:T(8,128)(2,1)} %param.9, bf16[512,8192]{1,0:T(8,128)(2,1)} %bitcast.22, bf16[7168,8192]{1,0:T(8,128)(2,1)} %all-gather.5.cloned.1.call-done), kind=kOutput, calls=%fused_computation.6.clone.clone.clone.1 | convolution fusion | flops 60155232256 | bytes 140509184 | tf_op jit(solution)/shard_map/dot_general | solution.py:8
  911.0 0.0 copy-start.3
  911.0 4.2 fusion.5
  915.2 0.0 all-reduce.3.cloned.1.call-update
  915.3 0.0 copy-done.3
  915.3 7.2 all_gather.11
  922.5 28.5 %all-reduce.3.cloned.1.call-done = (f32[512,64]{0,1:T(8,128)}, f32[512,64]{0,1:T(8,128)}) async-done(((f32[512,64]{0,1:T(8,128)}, f32[512,64]{0,1:T(8,128)}), (f32[512,64]{0,1:T(8,128)}, f32[512,64]{0,1:T(8,128)})) %all-reduce.3.cloned.1.call-update) | async-done | bytes 262160 | tf_op jit(solution)/shard_map/psum | solution.py:22
  951.0 2.4 multiply_convert_fusion
  953.3 1.5 convolution_bitcast_fusion
  954.8 0.0 copy-done.1
Async XLA Ops:
  6.5 1.6 copy-start
  6.5 154.2 %all-gather.3.cloned.1.call-start = ((), (), s32[]{:S(2)}) async-start(), calls=%async_computation | async-start | bytes 10485760 | tf_op jit(solution)/shard_map/all_gather | solution.py:16
  7.3 1.1 copy-start.2
  7.3 832.8 %all-gather.5.cloned.1.call-start = ((), (), s32[]{:S(2)}) async-start(), calls=%async_computation.1 | async-start | bytes 146800640 | tf_op jit(solution)/shard_map/all_gather | solution.py:19
  8.0 942.9 %all-reduce.3.cloned.1.call-start = ((), (), s32[]{:S(2)}) async-start(), calls=%async_computation.2 | async-start | bytes 524288 | tf_op jit(solution)/shard_map/psum | solution.py:22
  840.1 114.7 %copy-start.1 = (bf16[512,2048]{1,0:T(8,128)(2,1)S(1)}, bf16[512,2048]{1,0:T(8,128)(2,1)}, u32[]{:S(2)}) copy-start(bf16[512,2048]{1,0:T(8,128)(2,1)} %param.7) | copy-start | bytes 6291460
  911.0 4.3 copy-start.3
Sparse Core Ops, SparseCore 0:
  8.9 151.8 all-gather.2
  162.4 677.6 all-gather.4
  915.4 35.5 all-reduce.2
where the time goes:
time: 962 us; the launch traced here: 961 us
  waiting for transfers between devices  841 us (87%)
  matrix products  78 us (8%)
  local copies, waits for them, and re-layouts  19.6 us (2%)
  between operations  13.2 us (1%)
    all_gather x1, waiting for transfers between devices, on_device(): lax.all_gather(down_weight, 'dp', axis=1, tiled=True)  660 us
    all_gather x1, waiting for transfers between devices, on_device(): gathered = lax.all_gather(out_grad, 'tensor', axis=2, tiled=True)  151 us
    dot_general x2, matrix products, contract_last(): lax.dot_general(left, right, (((1,), (1,)), ((), ())), preferred_element_...  72.4 us
    psum x1, waiting for transfers between devices, on_device(): grad_proj = lax.psum(grad_part, 'tensor')  28.5 us
    unnamed x9, local copies, waits for them, and re-layouts  19.6 us
  transfers between devices with their start and end apart: 3, of which 3 were waited for; matrix products, arithmetic and copies ran while one was open for 2% of the time, Pallas kernels for 0%

commit v1 on v0

v1 whole, which is shorter than its diff:
```python
import functools

import jax
import jax.numpy as jnp
from jax import lax
from jax.experimental import pallas as pl
from jax.experimental.pallas import tpu as pltpu
from jax.sharding import PartitionSpec as P

LANES = 128
CHUNK = 1024
TILE = 512


def swap(value, axis, size, mask):
    return lax.ppermute(value, axis, [(i, i ^ mask) for i in range(size)])


def project_kernel(shards, grad_ref, gate_ref, weight_ref, proj_ref, out_ref):
    @pl.when(pl.program_id(0) == 0)
    def _():
        out_ref[...] = jnp.zeros_like(out_ref)

    width = grad_ref.shape[2]
    hidden = None
    for shard in range(shards):
        term = lax.dot_general(
            grad_ref[shard],
            weight_ref[:, shard * width : (shard + 1) * width],
            (((1,), (1,)), ((), ())),
            preferred_element_type=jnp.float32,
        )
        hidden = term if hidden is None else hidden + term
    gate = gate_ref[...].astype(jnp.float32)
    up_grad = (hidden * (gate / (1.0 + jnp.exp(-gate)))).astype(jnp.bfloat16)
    out_ref[...] += jnp.dot(up_grad, proj_ref[...], preferred_element_type=jnp.float32)


def project(grad, gate, weight, proj, offset, span, local_gate):
    shards, rows, width = grad.shape
    tile = TILE if span % TILE == 0 else span
    first = offset // tile
    gate_first = first if local_gate else 0
    return pl.pallas_call(
        functools.partial(project_kernel, shards),
        grid=(span // tile,),
        in_specs=[
            pl.BlockSpec((shards, rows, width), lambda i: (0, 0, 0)),
            pl.BlockSpec((rows, tile), lambda i: (0, gate_first + i)),
            pl.BlockSpec((tile, shards * width), lambda i: (first + i, 0)),
            pl.BlockSpec((tile, proj.shape[1]), lambda i: (first + i, 0)),
        ],
        out_specs=pl.BlockSpec((rows, proj.shape[1]), lambda i: (0, 0)),
        out_shape=jax.ShapeDtypeStruct((rows, proj.shape[1]), jnp.float32),
        compiler_params=pltpu.CompilerParams(vmem_limit_bytes=40 * 1024 * 1024),
        cost_estimate=pl.CostEstimate(
            flops=2 * rows * span * (shards * width + 4 * proj.shape[1]),
            bytes_accessed=2 * span * (shards * width + rows),
            transcendentals=rows * span,
        ),
    )(grad, gate, weight, proj)


def sum_over(value, axis, size):
    mask = 1
    while mask < size:
        value = value + swap(value, axis, size, mask)
        mask *= 2
    return value


def on_device(n_dp, n_tensor, inputs, out_grad, gate_pre, down_weight, proj_in, proj_out, queries):
    rows = out_grad.shape[0]
    hidden = gate_pre.shape[1]
    me = lax.axis_index("dp")
    far, near = n_dp // 2, 1

    chunk = CHUNK if hidden % CHUNK == 0 else hidden
    starts = list(range(0, hidden, chunk))

    def gather(block):
        grad = lax.all_gather(block, "tensor", axis=0, tiled=False)
        if block.shape[1] % LANES:
            grad = jnp.swapaxes(grad, 0, 1).reshape(1, rows, -1)
        return grad

    def own_block(mask):
        return lax.dynamic_index_in_dim(out_grad, me ^ mask, axis=1, keepdims=False)

    grads = []
    for mask in range(n_dp):
        block = own_block(mask)
        if mask:
            block = swap(block, "dp", n_dp, mask)
        grads.append(gather(block))

    far_gates = [swap(gate_pre[:, s : s + chunk], "dp", n_dp, far) for s in starts]
    near_gate = swap(gate_pre, "dp", n_dp, near)
    diag_gates = [swap(g, "dp", n_dp, near) for g in far_gates]

    input_part = jnp.dot(inputs, proj_in, preferred_element_type=jnp.float32)
    input_proj = sum_over(input_part, "tensor", n_tensor)

    far_query = swap(queries, "dp", n_dp, far)
    near_query = swap(queries, "dp", n_dp, near)
    diag_query = swap(far_query, "dp", n_dp, near)

    parts = [
        project(grads[0], gate_pre, down_weight, proj_out, 0, hidden, True),
        project(grads[1], near_gate, down_weight, proj_out, 0, hidden, True),
        0.0,
        0.0,
    ]
    for index, s in enumerate(starts):
        parts[2] += project(grads[2], far_gates[index], down_weight, proj_out, s, chunk, False)
        parts[3] += project(grads[3], diag_gates[index], down_weight, proj_out, s, chunk, False)

    grad_part = parts[0]
    for mask in range(1, n_dp):
        grad_part = grad_part + swap(parts[mask], "dp", n_dp, mask)
    grad_proj = sum_over(grad_part, "tensor", n_tensor)

    features = (
        (input_proj[:, :, None] * grad_proj[:, None, :]).reshape(rows, -1).astype(jnp.bfloat16)
    )
    width = queries.shape[1]
    all_queries = jnp.zeros((queries.shape[0], n_dp * width), queries.dtype)
    for mask, block in enumerate((queries, near_query, far_query, diag_query)):
        all_queries = lax.dynamic_update_slice(all_queries, block, (0, (me ^ mask) * width))
    return lax.dot_general(
        all_queries, features, (((1,), (1,)), ((), ())), preferred_element_type=jnp.float32
    )


def solution(mesh):
    return jax.shard_map(
        functools.partial(on_device, mesh.shape["dp"], mesh.shape["tensor"]),
        mesh=mesh,
        in_specs=(
            P(("parts", "dp"), "tensor"),
            P(("parts", "dp"), None, "tensor"),
            P(("parts", "dp"), "tensor"),
            P("tensor", "dp"),
            P("tensor", None),
            P("tensor", None),
            P("tensor", "dp"),
        ),
        out_specs=P("tensor", ("parts", "dp")),
        check_vma=False,
    )
```

time: 962 us -> 364 us (0.38)
  waiting for transfers between devices: 841 us -> 170 us
  Pallas kernels: 0 us -> 116 us
  matrix products: 78 us -> 2.92 us
  starting transfers between devices: 0.08 us -> 22.2 us
  local copies, waits for them, and re-layouts: 19.6 us -> 35.5 us
    all_gather x2 -> x4, waiting for transfers between devices: 811 us -> 0.03 us  [gather(): grad = lax.all_gather(block, 'tensor', axis=0, tiled=False)]
    ppermute x0 -> x28, waiting for transfers between devices: none -> 170 us  [swap(): return lax.ppermute(value, axis, [(i, i ^ mask) for i in range(size)])]
    pallas_call x0 -> x16, Pallas kernels: none -> 116 us  [project(): pl.pallas_call(functools.partial(project_kernel, shards), grid=(span // t...]
    dot_general x4 -> x2, matrix products: 78 us -> 2.92 us  [the longest x1 1.5 us: on_device(): lax.dot_general(all_queries, features, (((1,), (1,)), ((), ())), preferre...]
    psum x1 -> x0, waiting for transfers between devices: 28.5 us -> none  [on_device(): grad_proj = lax.psum(grad_part, 'tensor')]
    ppermute x0 -> x28, starting transfers between devices: none -> 22.1 us  [swap(): return lax.ppermute(value, axis, [(i, i ^ mask) for i in range(size)])]
    unnamed x9 -> x37, local copies, waits for them, and re-layouts: 19.6 us -> 18.1 us
  transfers between devices with their start and end apart: 3 -> 32, of which waited for: 3 -> 13; matrix products, arithmetic and copies ran while one was open for 2% -> 4% of each run, Pallas kernels for 0% -> 32%
where the time goes in v1:
time: 364 us; the launch traced here: 363 us
  waiting for transfers between devices  170 us (47%)
  Pallas kernels  116 us (32%)
  local copies, waits for them, and re-layouts  35.5 us (10%)
  starting transfers between devices  22.2 us (6%)
  between operations  13.6 us (4%)
    ppermute x28, waiting for transfers between devices, swap(): return lax.ppermute(value, axis, [(i, i ^ mask) for i in range(size)])  170 us
    pallas_call x16, Pallas kernels, project(): pl.pallas_call(functools.partial(project_kernel, shards), grid=(span // t...  116 us
    ppermute x28, starting transfers between devices, swap(): return lax.ppermute(value, axis, [(i, i ^ mask) for i in range(size)])  22.1 us
    unnamed x37, local copies, waits for them, and re-layouts  18.1 us
    dynamic_slice x1, local copies, waits for them, and re-layouts, own_block(): return lax.dynamic_index_in_dim(out_grad, me ^ mask, axis=1, keepdims=False)  9.26 us
  transfers between devices with their start and end apart: 32, of which 13 were waited for; matrix products, arithmetic and copies ran while one was open for 4% of the time, Pallas kernels for 32%

profile of v1, /device:TPU:0, one launch (start us, length us, event | category | flops | bytes accessed | tf_op | source)
XLA Modules:
  0.0 362.9 jit_solution(12975117412182065542)
XLA Ops:
  6.5 9.3 %constant_dynamic-slice_fusion.2 = (bf16[512,1,512]{2,1,0:T(2,128)(2,1)}, bf16[512,1,512]{2,1,0:T(2,128)(2,1)S(1)}, bf16[512,1,512]{2,1,0:T(2,128)(2,1)S(1)}, bf16[512,1,512]{2,1,0:T(2,128)(2,1)}) fusion(bf16[512,4,512]{2,1,0:T(4,128)(2,1)} %param.8, s32[]{:T(128)S(6)} %select_n.30, s32[]{:T(128)S(6)} %select_n.31, s32[]{:T(128)S(6)} %select_n.29, ...), kind=kLoop, calls=%fused_computation.9 | loop fusion | bytes 4194320 | tf_op jit(solution)/shard_map/jit(dynamic_index_in_dim)/dynamic_slice | solution.py:88
  15.9 3.0 collective-permute-start.8
  18.9 12.0 %collective-permute-done.8 = bf16[512,512]{1,0:T(8,128)(2,1)} collective-permute-done((bf16[512,512]{1,0:T(8,128)(2,1)S(1)}, bf16[512,512]{1,0:T(8,128)(2,1)}, u32[]{:S(2)}, u32[]{:S(2)}) %collective-permute-start.8) | collective-permute-done | bytes 524320 | tf_op jit(solution)/shard_map/ppermute | solution.py:16
  31.0 1.3 copy.53
  32.8 13.7 %collective-permute-done.17 = bf16[512,512]{1,0:T(8,128)(2,1)} collective-permute-done((bf16[512,512]{1,0:T(8,128)(2,1)S(1)}, bf16[512,512]{1,0:T(8,128)(2,1)}, u32[]{:S(2)}, u32[]{:S(2)}) %collective-permute-start.17) | collective-permute-done | bytes 524320 | tf_op jit(solution)/shard_map/ppermute | solution.py:16
  46.6 1.3 copy.55
  48.5 1.6 collective-permute-done.5
  50.1 6.2 %fusion = (bf16[512,1024]{1,0:T(8,128)(2,1)}, bf16[512,1024]{1,0:T(8,128)(2,1)}, bf16[512,1024]{1,0:T(8,128)(2,1)}, bf16[512,1024]{1,0:T(8,128)(2,1)}, bf16[512,...) fusion(bf16[512,7168]{1,0:T(8,128)(2,1)} %gate_ref.1), kind=kLoop, calls=%fused_computation.15 | loop fusion | bytes 14680064 | tf_op jit(solution)/shard_map/slice | solution.py:97
  56.3 1.2 collective-permute-start.9
  57.5 0.9 collective-permute-start.10
  58.3 1.2 collective-permute-start.11
  59.5 0.9 collective-permute-start.12
  60.4 22.0 %collective-permute-done.9.gate_ref = bf16[512,1024]{1,0:T(8,128)(2,1)} collective-permute-done((bf16[512,1024]{1,0:T(8,128)(2,1)S(1)}, bf16[512,1024]{1,0:T(8,128)(2,1)}, u32[]{:S(2)}, u32[]{:S(2)}) %collective-permute-start.9) | collective-permute-done | bytes 1048608 | tf_op jit(solution)/shard_map/ppermute | solution.py:16
  82.4 1.2 collective-permute-start.13
  83.6 0.9 copy.46
  84.5 20.3 %collective-permute-done.10.gate_ref = bf16[512,1024]{1,0:T(8,128)(2,1)} collective-permute-done((bf16[512,1024]{1,0:T(8,128)(2,1)}, bf16[512,1024]{1,0:T(8,128)(2,1)}, u32[]{:S(2)}, u32[]{:S(2)}) %collective-permute-start.10) | collective-permute-done | bytes 1048608 | tf_op jit(solution)/shard_map/ppermute | solution.py:16
  104.9 1.2 collective-permute-start.14
  106.1 1.4 fusion.1
  107.5 1.9 copy.26.proj_ref
  109.4 17.9 %collective-permute-done.11.gate_ref = bf16[512,1024]{1,0:T(8,128)(2,1)} collective-permute-done((bf16[512,1024]{1,0:T(8,128)(2,1)}, bf16[512,1024]{1,0:T(8,128)(2,1)}, u32[]{:S(2)}, u32[]{:S(2)}) %collective-permute-start.11) | collective-permute-done | bytes 1048608 | tf_op jit(solution)/shard_map/ppermute | solution.py:16
  127.3 1.2 collective-permute-start.15
  128.5 1.6 copy-done.3
  130.1 4.9 %shard_map.75 = f32[512,64]{1,0:T(8,128)S(1)} custom-call(bf16[4,512,512]{2,1,0:T(8,128)(2,1)S(1)} %bitcast.25, bf16[512,1024]{1,0:T(8,128)(2,1)} %collective-permute-done.9.gate_ref, bf16[7168,2048]{1,0:T(8,128)(2,1)} %weight_ref.31, bf16[7168,64]{1,0:T(8,128)(2,1)S(1)} %copy.26.proj_ref), custom_call_target="tpu_custom_call" | custom-call | flops 2415919104 | bytes 5242880 | tf_op jit(solution)/shard_map/pallas_call | solution.py:44
  135.1 14.7 %collective-permute-done.12.gate_ref = bf16[512,1024]{1,0:T(8,128)(2,1)} collective-permute-done((bf16[512,1024]{1,0:T(8,128)(2,1)}, bf16[512,1024]{1,0:T(8,128)(2,1)}, u32[]{:S(2)}, u32[]{:S(2)}) %collective-permute-start.12) | collective-permute-done | bytes 1048608 | tf_op jit(solution)/shard_map/ppermute | solution.py:16
  149.8 4.9 %shard_map.76 = f32[512,64]{1,0:T(8,128)S(1)} custom-call(bf16[4,512,512]{2,1,0:T(8,128)(2,1)S(1)} %bitcast.26, bf16[512,1024]{1,0:T(8,128)(2,1)} %collective-permute-done.10.gate_ref, bf16[7168,2048]{1,0:T(8,128)(2,1)} %weight_ref.31, bf16[7168,64]{1,0:T(8,128)(2,1)S(1)} %copy.26.proj_ref), custom_call_target="tpu_custom_call" | custom-call | flops 2415919104 | bytes 5242880 | tf_op jit(solution)/shard_map/pallas_call | solution.py:44
  154.7 4.9 %shard_map.77 = f32[512,64]{1,0:T(8,128)S(1)} custom-call(bf16[4,512,512]{2,1,0:T(8,128)(2,1)S(1)} %bitcast.27, bf16[512,1024]{1,0:T(8,128)(2,1)} %collective-permute-done.11.gate_ref, bf16[7168,2048]{1,0:T(8,128)(2,1)} %weight_ref.31, bf16[7168,64]{1,0:T(8,128)(2,1)S(1)} %copy.26.proj_ref), custom_call_target="tpu_custom_call" | custom-call | flops 2415919104 | bytes 5242880 | tf_op jit(solution)/shard_map/pallas_call | solution.py:44
  159.6 12.7 %collective-permute-done.13.gate_ref = bf16[512,1024]{1,0:T(8,128)(2,1)} collective-permute-done((bf16[512,1024]{1,0:T(8,128)(2,1)}, bf16[512,1024]{1,0:T(8,128)(2,1)}, u32[]{:S(2)}, u32[]{:S(2)}) %collective-permute-start.13) | collective-permute-done | bytes 1048608 | tf_op jit(solution)/shard_map/ppermute | solution.py:16
  172.3 4.9 %shard_map.78 = f32[512,64]{1,0:T(8,128)S(1)} custom-call(bf16[4,512,512]{2,1,0:T(8,128)(2,1)S(1)} %bitcast.28, bf16[512,1024]{1,0:T(8,128)(2,1)} %collective-permute-done.12.gate_ref, bf16[7168,2048]{1,0:T(8,128)(2,1)} %weight_ref.31, bf16[7168,64]{1,0:T(8,128)(2,1)S(1)} %copy.26.proj_ref), custom_call_target="tpu_custom_call" | custom-call | flops 2415919104 | bytes 5242880 | tf_op jit(solution)/shard_map/pallas_call | solution.py:44
  177.1 17.6 %collective-permute-done.14.gate_ref = bf16[512,1024]{1,0:T(8,128)(2,1)} collective-permute-done((bf16[512,1024]{1,0:T(8,128)(2,1)}, bf16[512,1024]{1,0:T(8,128)(2,1)}, u32[]{:S(2)}, u32[]{:S(2)}) %collective-permute-start.14) | collective-permute-done | bytes 1048608 | tf_op jit(solution)/shard_map/ppermute | solution.py:16
  194.7 4.9 %shard_map.79 = f32[512,64]{1,0:T(8,128)S(1)} custom-call(bf16[4,512,512]{2,1,0:T(8,128)(2,1)S(1)} %bitcast.29, bf16[512,1024]{1,0:T(8,128)(2,1)} %collective-permute-done.13.gate_ref, bf16[7168,2048]{1,0:T(8,128)(2,1)} %weight_ref.31, bf16[7168,64]{1,0:T(8,128)(2,1)S(1)} %copy.26.proj_ref), custom_call_target="tpu_custom_call" | custom-call | flops 2415919104 | bytes 5242880 | tf_op jit(solution)/shard_map/pallas_call | solution.py:44
  199.6 17.0 %collective-permute-done.15.gate_ref = bf16[512,1024]{1,0:T(8,128)(2,1)} collective-permute-done((bf16[512,1024]{1,0:T(8,128)(2,1)}, bf16[512,1024]{1,0:T(8,128)(2,1)}, u32[]{:S(2)}, u32[]{:S(2)}) %collective-permute-start.15) | collective-permute-done | bytes 1048608 | tf_op jit(solution)/shard_map/ppermute | solution.py:16
  216.6 4.9 %shard_map.80 = f32[512,64]{1,0:T(8,128)S(1)} custom-call(bf16[4,512,512]{2,1,0:T(8,128)(2,1)S(1)} %bitcast.30, bf16[512,1024]{1,0:T(8,128)(2,1)} %collective-permute-done.14.gate_ref, bf16[7168,2048]{1,0:T(8,128)(2,1)} %weight_ref.31, bf16[7168,64]{1,0:T(8,128)(2,1)S(1)} %copy.26.proj_ref), custom_call_target="tpu_custom_call" | custom-call | flops 2415919104 | bytes 5242880 | tf_op jit(solution)/shard_map/pallas_call | solution.py:44
  221.5 0.7 copy-done.5
  222.2 1.0 copy-done.9
  223.7 4.9 %shard_map.81 = f32[512,64]{1,0:T(8,128)S(1)} custom-call(bf16[4,512,512]{2,1,0:T(8,128)(2,1)S(1)} %bitcast.31, bf16[512,1024]{1,0:T(8,128)(2,1)} %collective-permute-done.15.gate_ref, bf16[7168,2048]{1,0:T(8,128)(2,1)} %weight_ref.31, bf16[7168,64]{1,0:T(8,128)(2,1)S(1)} %copy.26.proj_ref), custom_call_target="tpu_custom_call" | custom-call | flops 2415919104 | bytes 5242880 | tf_op jit(solution)/shard_map/pallas_call | solution.py:44
  228.7 1.7 copy-done.2
  230.3 1.2 copy-done.10
  231.6 4.7 %shard_map.82 = f32[512,64]{1,0:T(8,128)S(1)} custom-call(bf16[4,512,512]{2,1,0:T(8,128)(2,1)S(1)} %bitcast.18, bf16[512,1024]{1,0:T(8,128)(2,1)S(1)} %copy-done.10, bf16[7168,2048]{1,0:T(8,128)(2,1)} %weight_ref.31, bf16[7168,64]{1,0:T(8,128)(2,1)S(1)} %copy.26.proj_ref), custom_call_target="tpu_custom_call" | custom-call | flops 2415919104 | bytes 5242880 | tf_op jit(solution)/shard_map/pallas_call | solution.py:44
  236.4 4.9 %shard_map.83 = f32[512,64]{1,0:T(8,128)S(1)} custom-call(bf16[4,512,512]{2,1,0:T(8,128)(2,1)S(1)} %bitcast.19, bf16[512,1024]{1,0:T(8,128)(2,1)} %collective-permute-done.19.gate_ref, bf16[7168,2048]{1,0:T(8,128)(2,1)} %weight_ref.31, bf16[7168,64]{1,0:T(8,128)(2,1)S(1)} %copy.26.proj_ref), custom_call_target="tpu_custom_call" | custom-call | flops 2415919104 | bytes 5242880 | tf_op jit(solution)/shard_map/pallas_call | solution.py:44
  241.3 0.6 collective-permute-start.24
  241.8 4.9 %shard_map.84 = f32[512,64]{1,0:T(8,128)S(1)} custom-call(bf16[4,512,512]{2,1,0:T(8,128)(2,1)S(1)} %bitcast.20, bf16[512,1024]{1,0:T(8,128)(2,1)} %collective-permute-done.20.gate_ref, bf16[7168,2048]{1,0:T(8,128)(2,1)} %weight_ref.31, bf16[7168,64]{1,0:T(8,128)(2,1)S(1)} %copy.26.proj_ref), custom_call_target="tpu_custom_call" | custom-call | flops 2415919104 | bytes 5242880 | tf_op jit(solution)/shard_map/pallas_call | solution.py:44
  247.0 4.9 %shard_map.85 = f32[512,64]{1,0:T(8,128)S(1)} custom-call(bf16[4,512,512]{2,1,0:T(8,128)(2,1)S(1)} %bitcast.21, bf16[512,1024]{1,0:T(8,128)(2,1)} %collective-permute-done.21.gate_ref, bf16[7168,2048]{1,0:T(8,128)(2,1)} %weight_ref.31, bf16[7168,64]{1,0:T(8,128)(2,1)S(1)} %copy.26.proj_ref), custom_call_target="tpu_custom_call" | custom-call | flops 2415919104 | bytes 5242880 | tf_op jit(solution)/shard_map/pallas_call | solution.py:44
  252.0 1.0 collective-permute-start.1
  252.9 4.9 %shard_map.86 = f32[512,64]{1,0:T(8,128)S(1)} custom-call(bf16[4,512,512]{2,1,0:T(8,128)(2,1)S(1)} %bitcast.22, bf16[512,1024]{1,0:T(8,128)(2,1)} %collective-permute-done.22.gate_ref, bf16[7168,2048]{1,0:T(8,128)(2,1)} %weight_ref.31, bf16[7168,64]{1,0:T(8,128)(2,1)S(1)} %copy.26.proj_ref), custom_call_target="tpu_custom_call" | custom-call | flops 2415919104 | bytes 5242880 | tf_op jit(solution)/shard_map/pallas_call | solution.py:44
  257.9 1.2 collective-permute-start.16
  259.1 4.7 %shard_map.87 = f32[512,64]{1,0:T(8,128)S(1)} custom-call(bf16[4,512,512]{2,1,0:T(8,128)(2,1)S(1)} %bitcast.23, bf16[512,1024]{1,0:T(8,128)(2,1)S(1)} %collective-permute-done.23.gate_ref, bf16[7168,2048]{1,0:T(8,128)(2,1)} %weight_ref.31, bf16[7168,64]{1,0:T(8,128)(2,1)S(1)} %copy.26.proj_ref), custom_call_target="tpu_custom_call" | custom-call | flops 2415919104 | bytes 5242880 | tf_op jit(solution)/shard_map/pallas_call | solution.py:44
  263.8 4.7 %shard_map.88 = f32[512,64]{1,0:T(8,128)S(1)} custom-call(bf16[4,512,512]{2,1,0:T(8,128)(2,1)S(1)} %bitcast.24, bf16[512,1024]{1,0:T(8,128)(2,1)S(1)} %collective-permute-done.24.gate_ref, bf16[7168,2048]{1,0:T(8,128)(2,1)} %weight_ref.31, bf16[7168,64]{1,0:T(8,128)(2,1)S(1)} %copy.26.proj_ref), custom_call_target="tpu_custom_call" | custom-call | flops 2415919104 | bytes 5242880 | tf_op jit(solution)/shard_map/pallas_call | solution.py:44
  268.6 0.8 add_add_fusion
  269.6 1.6 copy-done.11
  271.2 24.8 %shard_map.74 = f32[512,64]{1,0:T(8,128)S(1)} custom-call(bf16[4,512,512]{2,1,0:T(8,128)(2,1)S(1)} %bitcast.32, bf16[512,7168]{1,0:T(8,128)(2,1)} %collective-permute-done.6.gate_ref, bf16[7168,2048]{1,0:T(8,128)(2,1)} %weight_ref.31, bf16[7168,64]{1,0:T(8,128)(2,1)S(1)} %copy.26.proj_ref), custom_call_target="tpu_custom_call" | custom-call | flops 16911433728 | bytes 36700160 | tf_op jit(solution)/shard_map/pallas_call | solution.py:44
  296.0 0.9 collective-permute-start.7
  296.9 3.1 copy-done.4
  300.0 1.6 copy-done.12
  301.6 23.7 %shard_map.73 = f32[512,64]{1,0:T(8,128)S(1)} custom-call(bf16[4,512,512]{2,1,0:T(8,128)(2,1)S(1)} %bitcast.33, bf16[512,7168]{1,0:T(8,128)(2,1)S(1)} %copy-done.4, bf16[7168,2048]{1,0:T(8,128)(2,1)} %weight_ref.31, bf16[7168,64]{1,0:T(8,128)(2,1)S(1)} %copy.26.proj_ref), custom_call_target="tpu_custom_call" | custom-call | flops 16911433728 | bytes 36700160 | tf_op jit(solution)/shard_map/pallas_call | solution.py:44
  325.3 1.7 collective-permute-start.3
  327.6 4.1 %collective-permute-done.3 = f32[512,64]{0,1:T(8,128)S(1)} collective-permute-done((f32[512,64]{0,1:T(8,128)S(1)}, f32[512,64]{0,1:T(8,128)S(1)}, u32[]{:S(2)}, u32[]{:S(2)}) %collective-permute-start.3) | collective-permute-done | bytes 131104 | tf_op jit(solution)/shard_map/ppermute | solution.py:16
  331.7 2.7 collective-permute-start.4
  334.4 0.9 constant_dynamic-update-slice_fusion.2
  335.4 3.9 %collective-permute-done.26 = f32[512,64]{1,0:T(8,128)S(1)} collective-permute-done((f32[512,64]{1,0:T(8,128)S(1)}, f32[512,64]{1,0:T(8,128)S(1)}, u32[]{:S(2)}, u32[]{:S(2)}) %collective-permute-start.26) | collective-permute-done | bytes 131104 | tf_op jit(solution)/shard_map/ppermute | solution.py:16
  339.3 0.9 collective-permute-start.27
  340.2 0.9 constant_dynamic-update-slice_fusion.1
  341.1 12.1 %collective-permute-done.27 = f32[512,64]{1,0:T(8,128)S(1)} collective-permute-done((f32[512,64]{1,0:T(8,128)S(1)}, f32[512,64]{1,0:T(8,128)S(1)}, u32[]{:S(2)}, u32[]{:S(2)}) %collective-permute-start.27) | collective-permute-done | bytes 131104 | tf_op jit(solution)/shard_map/ppermute | solution.py:16
  353.4 1.4 multiply_convert_fusion
  354.8 1.5 fusion.2
  (75 shorter events, 3.4 us)
Async XLA Ops:
  6.5 99.5 %copy-start = (bf16[512,2048]{1,0:T(8,128)(2,1)S(1)}, bf16[512,2048]{1,0:T(8,128)(2,1)}, u32[]{:S(2)}) copy-start(bf16[512,2048]{1,0:T(8,128)(2,1)} %param.7) | copy-start | bytes 6291460
  6.5 122.0 %all-gather.13.cloned.1.call-start = ((), (), s32[]{:S(2)}) async-start(), calls=%async_computation.2 | async-start | bytes 2621440 | tf_op jit(solution)/shard_map/all_gather | solution.py:82
  15.9 15.0 %collective-permute-start.8 = (bf16[512,512]{1,0:T(8,128)(2,1)S(1)}, bf16[512,512]{1,0:T(8,128)(2,1)}, u32[]{:S(2)}, u32[]{:S(2)}) collective-permute-start(bf16[512,512]{1,0:T(8,128)(2,1)S(1)} %bitcast.36), channel_id=1, source_target_pairs={{0,2},{1,3},{2,0},{3,1},{4,6},{5,7},{6,4},{7,5},{8,10},{9,11},{10,... | collective-permute-start | bytes 1572872 | tf_op jit(solution)/shard_map/ppermute | solution.py:16
  31.0 197.7 %all-gather.15.cloned.1.call-start = ((), (), s32[]{:S(2)}) async-start(), calls=%async_computation.3 | async-start | bytes 2621440 | tf_op jit(solution)/shard_map/all_gather | solution.py:82
  32.4 14.1 %collective-permute-start.17 = (bf16[512,512]{1,0:T(8,128)(2,1)S(1)}, bf16[512,512]{1,0:T(8,128)(2,1)}, u32[]{:S(2)}, u32[]{:S(2)}) collective-permute-start(bf16[512,512]{1,0:T(8,128)(2,1)S(1)} %bitcast.37), channel_id=1, source_target_pairs={{0,3},{1,2},{2,1},{3,0},{4,7},{5,6},{6,5},{7,4},{8,11},{9,10},{10,... | collective-permute-start | bytes 1572872 | tf_op jit(solution)/shard_map/ppermute | solution.py:16
  46.5 223.1 %all-gather.11.cloned.1.call-start = ((), (), s32[]{:S(2)}) async-start(), calls=%async_computation.1 | async-start | bytes 2621440 | tf_op jit(solution)/shard_map/all_gather | solution.py:82
  47.9 2.1 collective-permute-start.5
  48.4 221.2 %collective-permute-start.6 = (bf16[512,7168]{1,0:T(8,128)(2,1)}, bf16[512,7168]{1,0:T(8,128)(2,1)}, u32[]{:S(2)}, u32[]{:S(2)}) collective-permute-start(bf16[512,7168]{1,0:T(8,128)(2,1)} %gate_ref.1), channel_id=1, source_target_pairs={{0,1},{1,0},{2,3},{3,2},{4,5},{5,4},{6,7},{7,6},{8,9},{9,8},{10,11... | collective-permute-start | bytes 22020104 | tf_op jit(solution)/shard_map/ppermute | solution.py:16
  50.1 56.0 %copy-start.14 = (bf16[2048,64]{0,1:T(8,128)(2,1)S(1)}, bf16[2048,64]{0,1:T(8,128)(2,1)}, u32[]{:S(2)}) copy-start(bf16[2048,64]{0,1:T(8,128)(2,1)} %param.11) | copy-start | bytes 786436
  50.1 246.8 %all-gather.9.cloned.1.call-start = ((), (), s32[]{:S(2)}) async-start(), calls=%async_computation | async-start | bytes 2621440 | tf_op jit(solution)/shard_map/all_gather | solution.py:82
  56.3 26.1 %collective-permute-start.9 = (bf16[512,1024]{1,0:T(8,128)(2,1)S(1)}, bf16[512,1024]{1,0:T(8,128)(2,1)}, u32[]{:S(2)}, u32[]{:S(2)}) collective-permute-start(bf16[512,1024]{1,0:T(8,128)(2,1)S(1)} %get-tuple-element.9), channel_id=1, source_target_pairs={{0,2},{1,3},{2,0},{3,1},{4,6},{5,7},{6,4},{7,5},{8,10},{9,11},{10,... | collective-permute-start | bytes 3145736 | tf_op jit(solution)/shard_map/ppermute | solution.py:16
  57.5 47.4 %collective-permute-start.10 = (bf16[512,1024]{1,0:T(8,128)(2,1)}, bf16[512,1024]{1,0:T(8,128)(2,1)}, u32[]{:S(2)}, u32[]{:S(2)}) collective-permute-start(bf16[512,1024]{1,0:T(8,128)(2,1)} %get-tuple-element.5), channel_id=1, source_target_pairs={{0,2},{1,3},{2,0},{3,1},{4,6},{5,7},{6,4},{7,5},{8,10},{9,11},{10,... | collective-permute-start | bytes 3145736 | tf_op jit(solution)/shard_map/ppermute | solution.py:16
  58.3 69.0 %collective-permute-start.11 = (bf16[512,1024]{1,0:T(8,128)(2,1)}, bf16[512,1024]{1,0:T(8,128)(2,1)}, u32[]{:S(2)}, u32[]{:S(2)}) collective-permute-start(bf16[512,1024]{1,0:T(8,128)(2,1)} %get-tuple-element.8), channel_id=1, source_target_pairs={{0,2},{1,3},{2,0},{3,1},{4,6},{5,7},{6,4},{7,5},{8,10},{9,11},{10,... | collective-permute-start | bytes 3145736 | tf_op jit(solution)/shard_map/ppermute | solution.py:16
  59.5 90.3 %collective-permute-start.12 = (bf16[512,1024]{1,0:T(8,128)(2,1)}, bf16[512,1024]{1,0:T(8,128)(2,1)}, u32[]{:S(2)}, u32[]{:S(2)}) collective-permute-start(bf16[512,1024]{1,0:T(8,128)(2,1)} %get-tuple-element.7), channel_id=1, source_target_pairs={{0,2},{1,3},{2,0},{3,1},{4,6},{5,7},{6,4},{7,5},{8,10},{9,11},{10,... | collective-permute-start | bytes 3145736 | tf_op jit(solution)/shard_map/ppermute | solution.py:16
  82.4 89.9 %collective-permute-start.13 = (bf16[512,1024]{1,0:T(8,128)(2,1)}, bf16[512,1024]{1,0:T(8,128)(2,1)}, u32[]{:S(2)}, u32[]{:S(2)}) collective-permute-start(bf16[512,1024]{1,0:T(8,128)(2,1)} %get-tuple-element.6), channel_id=1, source_target_pairs={{0,2},{1,3},{2,0},{3,1},{4,6},{5,7},{6,4},{7,5},{8,10},{9,11},{10,... | collective-permute-start | bytes 3145736 | tf_op jit(solution)/shard_map/ppermute | solution.py:16
  104.9 89.9 %collective-permute-start.14 = (bf16[512,1024]{1,0:T(8,128)(2,1)}, bf16[512,1024]{1,0:T(8,128)(2,1)}, u32[]{:S(2)}, u32[]{:S(2)}) collective-permute-start(bf16[512,1024]{1,0:T(8,128)(2,1)} %get-tuple-element.11), channel_id=1, source_target_pairs={{0,2},{1,3},{2,0},{3,1},{4,6},{5,7},{6,4},{7,5},{8,10},{9,11},{10,... | collective-permute-start | bytes 3145736 | tf_op jit(solution)/shard_map/ppermute | solution.py:16
  127.3 89.3 %collective-permute-start.15 = (bf16[512,1024]{1,0:T(8,128)(2,1)}, bf16[512,1024]{1,0:T(8,128)(2,1)}, u32[]{:S(2)}, u32[]{:S(2)}) collective-permute-start(bf16[512,1024]{1,0:T(8,128)(2,1)} %get-tuple-element.10), channel_id=1, source_target_pairs={{0,2},{1,3},{2,0},{3,1},{4,6},{5,7},{6,4},{7,5},{8,10},{9,11},{10,... | collective-permute-start | bytes 3145736 | tf_op jit(solution)/shard_map/ppermute | solution.py:16
  128.5 1.6 copy-start.3
  149.8 72.4 %collective-permute-start.18 = (bf16[512,1024]{1,0:T(8,128)(2,1)}, bf16[512,1024]{1,0:T(8,128)(2,1)S(1)}, u32[]{:S(2)}, u32[]{:S(2)}) collective-permute-start(bf16[512,1024]{1,0:T(8,128)(2,1)} %collective-permute-done.9.gate_ref), channel_id=1, source_target_pairs={{0,1},{1,0},{2,3},{3,2},{4,5},{5,4},{6,7},{7,6},{8,9},{9,8},{10,11... | collective-permute-start | bytes 3145736 | tf_op jit(solution)/shard_map/ppermute | solution.py:16
  172.3 64.0 %collective-permute-start.19 = (bf16[512,1024]{1,0:T(8,128)(2,1)}, bf16[512,1024]{1,0:T(8,128)(2,1)}, u32[]{:S(2)}, u32[]{:S(2)}) collective-permute-start(bf16[512,1024]{1,0:T(8,128)(2,1)} %collective-permute-done.10.gate_ref), channel_id=1, source_target_pairs={{0,1},{1,0},{2,3},{3,2},{4,5},{5,4},{6,7},{7,6},{8,9},{9,8},{10,11... | collective-permute-start | bytes 3145736 | tf_op jit(solution)/shard_map/ppermute | solution.py:16
  194.7 46.5 %collective-permute-start.20 = (bf16[512,1024]{1,0:T(8,128)(2,1)}, bf16[512,1024]{1,0:T(8,128)(2,1)}, u32[]{:S(2)}, u32[]{:S(2)}) collective-permute-start(bf16[512,1024]{1,0:T(8,128)(2,1)} %collective-permute-done.11.gate_ref), channel_id=1, source_target_pairs={{0,1},{1,0},{2,3},{3,2},{4,5},{5,4},{6,7},{7,6},{8,9},{9,8},{10,11... | collective-permute-start | bytes 3145736 | tf_op jit(solution)/shard_map/ppermute | solution.py:16
  216.6 30.1 %collective-permute-start.21 = (bf16[512,1024]{1,0:T(8,128)(2,1)}, bf16[512,1024]{1,0:T(8,128)(2,1)}, u32[]{:S(2)}, u32[]{:S(2)}) collective-permute-start(bf16[512,1024]{1,0:T(8,128)(2,1)} %collective-permute-done.12.gate_ref), channel_id=1, source_target_pairs={{0,1},{1,0},{2,3},{3,2},{4,5},{5,4},{6,7},{7,6},{8,9},{9,8},{10,11... | collective-permute-start | bytes 3145736 | tf_op jit(solution)/shard_map/ppermute | solution.py:16
  221.5 0.7 copy-start.5
  222.2 1.0 copy-start.9
  223.2 28.7 %collective-permute-start.22 = (bf16[512,1024]{1,0:T(8,128)(2,1)}, bf16[512,1024]{1,0:T(8,128)(2,1)}, u32[]{:S(2)}, u32[]{:S(2)}) collective-permute-start(bf16[512,1024]{1,0:T(8,128)(2,1)} %collective-permute-done.13.gate_ref), channel_id=1, source_target_pairs={{0,1},{1,0},{2,3},{3,2},{4,5},{5,4},{6,7},{7,6},{8,9},{9,8},{10,11... | collective-permute-start | bytes 3145736 | tf_op jit(solution)/shard_map/ppermute | solution.py:16
  228.6 7.7 %copy-start.7 = (f32[512,64]{1,0:T(8,128)}, f32[512,64]{1,0:T(8,128)S(1)}, u32[]{:S(2)}) copy-start(f32[512,64]{1,0:T(8,128)S(1)} %shard_map.81) | copy-start | bytes 393220
  228.7 1.7 copy-start.2
  230.3 1.2 copy-start.10
  236.3 21.6 %collective-permute-start.23 = (bf16[512,1024]{1,0:T(8,128)(2,1)}, bf16[512,1024]{1,0:T(8,128)(2,1)S(1)}, u32[]{:S(2)}, u32[]{:S(2)}) collective-permute-start(bf16[512,1024]{1,0:T(8,128)(2,1)} %collective-permute-done.14.gate_ref), channel_id=1, source_target_pairs={{0,1},{1,0},{2,3},{3,2},{4,5},{5,4},{6,7},{7,6},{8,9},{9,8},{10,11... | collective-permute-start | bytes 3145736 | tf_op jit(solution)/shard_map/ppermute | solution.py:16
  241.3 5.5 %copy-start.15 = (bf16[64,1024]{1,0:T(8,128)(2,1)S(1)}, bf16[64,1024]{1,0:T(8,128)(2,1)}, u32[]{:S(2)}) copy-start(bf16[64,1024]{1,0:T(8,128)(2,1)} %param.13) | copy-start | bytes 393220
  241.3 22.6 %collective-permute-start.24 = (bf16[512,1024]{1,0:T(8,128)(2,1)}, bf16[512,1024]{1,0:T(8,128)(2,1)S(1)}, u32[]{:S(2)}, u32[]{:S(2)}) collective-permute-start(bf16[512,1024]{1,0:T(8,128)(2,1)} %collective-permute-done.15.gate_ref), channel_id=1, source_target_pairs={{0,1},{1,0},{2,3},{3,2},{4,5},{5,4},{6,7},{7,6},{8,9},{9,8},{10,11... | collective-permute-start | bytes 3145736 | tf_op jit(solution)/shard_map/ppermute | solution.py:16
  246.7 87.7 %collective-permute-start = (bf16[64,1024]{1,0:T(8,128)(2,1)S(1)}, bf16[64,1024]{1,0:T(8,128)(2,1)}, u32[]{:S(2)}, u32[]{:S(2)}) collective-permute-start(bf16[64,1024]{1,0:T(8,128)(2,1)S(1)} %copy-done.15), channel_id=1, source_target_pairs={{0,1},{1,0},{2,3},{3,2},{4,5},{5,4},{6,7},{7,6},{8,9},{9,8},{10,11... | collective-permute-start | bytes 393224 | tf_op jit(solution)/shard_map/ppermute | solution.py:16
  251.9 5.9 %copy-start.6 = (f32[512,64]{1,0:T(8,128)S(1)}, f32[512,64]{1,0:T(8,128)}, u32[]{:S(2)}) copy-start(f32[512,64]{1,0:T(8,128)} %copy-done.5) | copy-start | bytes 393220
  251.9 5.9 %copy-start.8 = (f32[512,64]{1,0:T(8,128)S(1)}, f32[512,64]{1,0:T(8,128)}, u32[]{:S(2)}) copy-start(f32[512,64]{1,0:T(8,128)} %copy-done.7) | copy-start | bytes 393220
  252.0 82.5 %collective-permute-start.1 = (bf16[64,1024]{1,0:T(8,128)(2,1)S(1)}, bf16[64,1024]{1,0:T(8,128)(2,1)}, u32[]{:S(2)}, u32[]{:S(2)}) collective-permute-start(bf16[64,1024]{1,0:T(8,128)(2,1)S(1)} %copy-done.15), channel_id=1, source_target_pairs={{0,2},{1,3},{2,0},{3,1},{4,6},{5,7},{6,4},{7,5},{8,10},{9,11},{10,... | collective-permute-start | bytes 393224 | tf_op jit(solution)/shard_map/ppermute | solution.py:16
  257.9 67.3 %collective-permute-start.16 = (f32[512,64]{1,0:T(8,128)S(1)}, f32[512,64]{1,0:T(8,128)S(1)}, u32[]{:S(2)}, u32[]{:S(2)}) collective-permute-start(f32[512,64]{1,0:T(8,128)S(1)} %add_add_fusion.2), channel_id=1, source_target_pairs={{0,2},{1,3},{2,0},{3,1},{4,6},{5,7},{6,4},{7,5},{8,10},{9,11},{10,... | collective-permute-start | bytes 393224 | tf_op jit(solution)/shard_map/ppermute | solution.py:16
  269.4 57.6 %collective-permute-start.25 = (f32[512,64]{1,0:T(8,128)}, f32[512,64]{1,0:T(8,128)S(1)}, u32[]{:S(2)}, u32[]{:S(2)}) collective-permute-start(f32[512,64]{1,0:T(8,128)} %add_add_fusion), channel_id=1, source_target_pairs={{0,3},{1,2},{2,1},{3,0},{4,7},{5,6},{6,5},{7,4},{8,11},{9,10},{10,... | collective-permute-start | bytes 393224 | tf_op jit(solution)/shard_map/ppermute | solution.py:16
  269.6 1.6 copy-start.11
  296.0 31.0 %collective-permute-start.7 = (f32[512,64]{1,0:T(8,128)S(1)}, f32[512,64]{1,0:T(8,128)S(1)}, u32[]{:S(2)}, u32[]{:S(2)}) collective-permute-start(f32[512,64]{1,0:T(8,128)S(1)} %shard_map.74), channel_id=1, source_target_pairs={{0,1},{1,0},{2,3},{3,2},{4,5},{5,4},{6,7},{7,6},{8,9},{9,8},{10,11... | collective-permute-start | bytes 393224 | tf_op jit(solution)/shard_map/ppermute | solution.py:16
  296.9 3.1 copy-start.4
  300.0 1.6 copy-start.12
  301.6 23.7 %copy-start.13 = (f32[512,64]{0,1:T(8,128)S(1)}, f32[512,64]{0,1:T(8,128)}, u32[]{:S(2)}) copy-start(f32[512,64]{0,1:T(8,128)} %fusion.1) | copy-start | bytes 393220
  325.3 6.4 %collective-permute-start.3 = (f32[512,64]{0,1:T(8,128)S(1)}, f32[512,64]{0,1:T(8,128)S(1)}, u32[]{:S(2)}, u32[]{:S(2)}) collective-permute-start(f32[512,64]{0,1:T(8,128)S(1)} %copy-done.13), channel_id=1, source_target_pairs={{0,4},{4,0},{8,12},{12,8},{1,5},{5,1},{9,13},{13,9},{2,6},{6,2},{1... | collective-permute-start | bytes 393224 | tf_op jit(solution)/shard_map/ppermute | solution.py:16
  327.0 12.2 %collective-permute-start.26 = (f32[512,64]{1,0:T(8,128)S(1)}, f32[512,64]{1,0:T(8,128)S(1)}, u32[]{:S(2)}, u32[]{:S(2)}) collective-permute-start(f32[512,64]{1,0:T(8,128)S(1)} %add_add_fusion.1), channel_id=1, source_target_pairs={{0,4},{4,0},{8,12},{12,8},{1,5},{5,1},{9,13},{13,9},{2,6},{6,2},{1... | collective-permute-start | bytes 393224 | tf_op jit(solution)/shard_map/ppermute | solution.py:16
  331.7 9.3 %collective-permute-start.4 = (f32[512,64]{0,1:T(8,128)S(1)}, f32[512,64]{0,1:T(8,128)S(1)}, u32[]{:S(2)}, u32[]{:S(2)}) collective-permute-start(f32[512,64]{0,1:T(8,128)S(1)} %add.86), channel_id=1, source_target_pairs={{0,8},{4,12},{8,0},{12,4},{1,9},{5,13},{9,1},{13,5},{2,10},{6,14},... | collective-permute-start | bytes 393224 | tf_op jit(solution)/shard_map/ppermute | solution.py:16
  334.4 6.7 %collective-permute-start.2 = (bf16[64,1024]{1,0:T(8,128)(2,1)}, bf16[64,1024]{1,0:T(8,128)(2,1)S(1)}, u32[]{:S(2)}, u32[]{:S(2)}) collective-permute-start(bf16[64,1024]{1,0:T(8,128)(2,1)} %collective-permute-done.1), channel_id=1, source_target_pairs={{0,1},{1,0},{2,3},{3,2},{4,5},{5,4},{6,7},{7,6},{8,9},{9,8},{10,11... | collective-permute-start | bytes 393224 | tf_op jit(solution)/shard_map/ppermute | solution.py:16
  339.3 14.0 %collective-permute-start.27 = (f32[512,64]{1,0:T(8,128)S(1)}, f32[512,64]{1,0:T(8,128)S(1)}, u32[]{:S(2)}, u32[]{:S(2)}) collective-permute-start(f32[512,64]{1,0:T(8,128)S(1)} %add.107), channel_id=1, source_target_pairs={{0,8},{4,12},{8,0},{12,4},{1,9},{5,13},{9,1},{13,5},{2,10},{6,14},... | collective-permute-start | bytes 393224 | tf_op jit(solution)/shard_map/ppermute | solution.py:16
  353.3 3.0 copy-start.1
Sparse Core Ops, SparseCore 0:
  31.1 47.4 all-gather.12
  80.1 44.6 all-gather.14
  126.4 44.5 all-gather.10
  172.5 44.8 all-gather.8

commit v2 on v1

v2 whole, which is shorter than its diff:
```python
import functools

import jax
import jax.numpy as jnp
from jax import lax
from jax.experimental import pallas as pl
from jax.experimental.pallas import tpu as pltpu
from jax.sharding import PartitionSpec as P

LANES = 128
UNIT = 512
SUB = 256
VMEM = 60 * 1024 * 1024


def swap(value, axis, size, mask):
    return lax.ppermute(value, axis, [(i, i ^ mask) for i in range(size)])


def split_kernel(grad_ref, out_ref):
    me = lax.axis_index("dp")
    blocks = [grad_ref[:, k, :] for k in range(grad_ref.shape[1])]
    bit = 1
    while bit < len(blocks):
        flip = (me & bit) != 0
        blocks = [jnp.where(flip, blocks[k ^ bit], blocks[k]) for k in range(len(blocks))]
        bit *= 2
    for k, block in enumerate(blocks):
        out_ref[k] = block


def split_blocks(out_grad):
    rows, n, width = out_grad.shape
    step = rows // 4
    return pl.pallas_call(
        split_kernel,
        grid=(4,),
        in_specs=[pl.BlockSpec((step, n, width), lambda i: (i, 0, 0))],
        out_specs=pl.BlockSpec((n, step, width), lambda i: (0, i, 0)),
        out_shape=jax.ShapeDtypeStruct((n, rows, width), out_grad.dtype),
        compiler_params=pltpu.CompilerParams(vmem_limit_bytes=VMEM),
        name="split_blocks",
    )(out_grad)


def project_kernel(sub, grad_ref, gate_ref, own_ref, near_ref, proj_ref, *refs):
    out_ref, rows_ref, sems = refs[-3:]
    shards, pair, _, width = grad_ref.shape

    @pl.when(pl.program_id(0) == 0)
    def _():
        copies = [
            pltpu.make_async_copy(
                grad_ref.at[s, p], rows_ref.at[p, :, s * width : (s + 1) * width], sems.at[s, p]
            )
            for s in range(shards)
            for p in range(pair)
        ]
        for copy in copies:
            copy.start()
        out_ref[...] = jnp.zeros_like(out_ref)
        for copy in copies:
            copy.wait()

    total = out_ref[...]
    for start in range(0, gate_ref.shape[1], sub):
        hidden = None
        for p, weight_ref in enumerate((own_ref, near_ref)):
            term = lax.dot_general(
                rows_ref[p],
                weight_ref[start : start + sub, :],
                (((1,), (1,)), ((), ())),
                preferred_element_type=jnp.float32,
            )
            hidden = term if hidden is None else hidden + term
        gate = gate_ref[:, start : start + sub].astype(jnp.float32)
        below = 1.0 + jnp.exp(-gate)
        inverse = pl.reciprocal(below, approx=True)
        inverse = inverse * (2.0 - below * inverse)
        up_grad = (hidden * (gate * inverse)).astype(jnp.bfloat16)
        total += jnp.dot(
            up_grad, proj_ref[start : start + sub, :], preferred_element_type=jnp.float32
        )
    out_ref[...] = total


def project(grad, gate, weights, proj, offset, span, gate_row, gate_column, after):
    shards, pair, rows, width = grad.shape
    tile = UNIT if span % UNIT == 0 else span
    sub = SUB if tile % SUB == 0 else tile
    first = offset // tile
    gate_first = gate_column // tile
    gate_block = gate_row // rows
    depth = shards * width
    return pl.pallas_call(
        functools.partial(project_kernel, sub),
        grid=(span // tile,),
        in_specs=[
            pl.BlockSpec(memory_space=pl.ANY),
            pl.BlockSpec((rows, tile), lambda i: (gate_block, gate_first + i)),
            pl.BlockSpec((tile, depth), lambda i: (first + i, 0)),
            pl.BlockSpec((tile, depth), lambda i: (first + i, 0)),
            pl.BlockSpec((tile, proj.shape[1]), lambda i: (first + i, 0)),
        ]
        + [pl.BlockSpec(memory_space=pl.ANY)] * len(after),
        out_specs=pl.BlockSpec((rows, proj.shape[1]), lambda i: (0, 0)),
        out_shape=jax.ShapeDtypeStruct((rows, proj.shape[1]), jnp.float32),
        scratch_shapes=[
            pltpu.VMEM((pair, rows, depth), grad.dtype),
            pltpu.SemaphoreType.DMA((shards, pair)),
        ],
        compiler_params=pltpu.CompilerParams(vmem_limit_bytes=VMEM),
        cost_estimate=pl.CostEstimate(
            flops=2 * rows * span * (pair * depth + 4 * proj.shape[1]),
            bytes_accessed=2 * span * (pair * depth + rows),
            transcendentals=rows * span,
        ),
        name="project",
    )(grad, gate, *weights, proj, *after)


def sum_over(value, axis, size):
    mask = 1
    while mask < size:
        value = value + swap(value, axis, size, mask)
        mask *= 2
    return value


def chunks_of(hidden):
    units = hidden // UNIT
    if hidden % UNIT or units < 8:
        return [(0, hidden)]
    cuts = [0] + [max(1, round(units * part)) for part in (2 / 7, 4 / 7, 11 / 14)] + [units - 1, units]
    return [(a * UNIT, (b - a) * UNIT) for a, b in zip(cuts, cuts[1:]) if b > a]


def on_device(n_dp, n_tensor, inputs, out_grad, gate_pre, down_weight, proj_in, proj_out, queries):
    rows = out_grad.shape[0]
    half = rows // 2
    hidden = gate_pre.shape[1]
    me = lax.axis_index("dp")
    far, near = n_dp // 2, 1

    def gather(block):
        grad = lax.all_gather(block, "tensor", axis=0, tiled=False)
        if block.shape[2] % LANES:
            grad = jnp.transpose(grad, (1, 2, 0, 3)).reshape(1, 2, block.shape[1], -1)
        return grad

    chunks = chunks_of(hidden)
    far_gates = [swap(gate_pre[:, s : s + n], "dp", n_dp, far) for s, n in chunks]

    blocks = split_blocks(out_grad)
    far_blocks = swap(blocks[2:], "dp", n_dp, far)
    grads_a = gather(blocks[:2, :half])
    grads_far = gather(far_blocks)
    grads_b = gather(blocks[:2, half:])

    weights = (down_weight, swap(down_weight, "dp", n_dp, near))

    input_part = jnp.dot(inputs, proj_in, preferred_element_type=jnp.float32)
    input_proj = sum_over(input_part, "tensor", n_tensor)

    far_query = swap(queries, "dp", n_dp, far)
    near_query = swap(queries, "dp", n_dp, near)
    diag_query = swap(far_query, "dp", n_dp, near)

    width = queries.shape[1]
    all_queries = jnp.zeros((queries.shape[0], n_dp * width), queries.dtype)
    for mask, block in enumerate((queries, near_query, far_query, diag_query)):
        all_queries = lax.dynamic_update_slice(all_queries, block, (0, (me ^ mask) * width))

    own_a = project(grads_a, gate_pre, weights, proj_out, 0, hidden, 0, 0, (input_proj,))
    after = (own_a, all_queries)
    far_sum = None
    own_b = None
    for index, (s, n) in enumerate(chunks):
        if index == len(chunks) - 1:
            own_b = project(grads_b, gate_pre, weights, proj_out, 0, hidden, half, 0, after)
            after = (own_b,)
        part = project(grads_far, far_gates[index], weights, proj_out, s, n, 0, 0, after)
        far_sum = part if far_sum is None else far_sum + part
        after = (part,)

    grad_part = jnp.concatenate([own_a, own_b]) + swap(far_sum, "dp", n_dp, far)
    grad_proj = sum_over(grad_part, "tensor", n_tensor)

    features = (
        (input_proj[:, :, None] * grad_proj[:, None, :]).reshape(rows, -1).astype(jnp.bfloat16)
    )
    return lax.dot_general(
        all_queries, features, (((1,), (1,)), ((), ())), preferred_element_type=jnp.float32
    )


def solution(mesh):
    return jax.shard_map(
        functools.partial(on_device, mesh.shape["dp"], mesh.shape["tensor"]),
        mesh=mesh,
        in_specs=(
            P(("parts", "dp"), "tensor"),
            P(("parts", "dp"), None, "tensor"),
            P(("parts", "dp"), "tensor"),
            P("tensor", "dp"),
            P("tensor", None),
            P("tensor", None),
            P("tensor", "dp"),
        ),
        out_specs=P("tensor", ("parts", "dp")),
        check_vma=False,
    )
```

time: 364 us -> 333 us (0.915)
  waiting for transfers between devices: 170 us -> 91.6 us
  Pallas kernels: 116 us -> 187 us
  local copies, waits for them, and re-layouts: 35.5 us -> 20.7 us
  starting transfers between devices: 22.2 us -> 14.3 us
    ppermute x28 -> x15, waiting for transfers between devices: 170 us -> 87.1 us  [swap(): return lax.ppermute(value, axis, [(i, i ^ mask) for i in range(size)])]
    pallas_call x16 -> x8, Pallas kernels: 116 us -> 187 us  [the longest x7 180 us: project(): pl.pallas_call(functools.partial(project_kernel, sub), grid=(span // tile...]
    unnamed x37 -> x35, local copies, waits for them, and re-layouts: 18.1 us -> 4.91 us
    slice x1 -> x6, local copies, waits for them, and re-layouts: 6.15 us -> 15.4 us  [the longest x4 11.9 us: on_device(): far_gates = [swap(gate_pre[:, s:s + n], 'dp', n_dp, far) for s, n in chunks]]
    dynamic_slice x1 -> x0, local copies, waits for them, and re-layouts: 9.26 us -> none  [own_block(): return lax.dynamic_index_in_dim(out_grad, me ^ mask, axis=1, keepdims=False)]
    ppermute x28 -> x15, starting transfers between devices: 22.1 us -> 14.2 us  [swap(): return lax.ppermute(value, axis, [(i, i ^ mask) for i in range(size)])]
    all_gather x4 -> x3, waiting for transfers between devices: 0.03 us -> 4.44 us  [gather(): grad = lax.all_gather(block, 'tensor', axis=0, tiled=False)]
  transfers between devices with their start and end apart: 32 -> 18, of which waited for: 13 -> 7; matrix products, arithmetic and copies ran while one was open for 4% -> 6% of each run, Pallas kernels for 32% -> 53%
where the time goes in v2:
time: 333 us
  Pallas kernels  187 us (56%)
  waiting for transfers between devices  91.6 us (28%)
  local copies, waits for them, and re-layouts  20.7 us (6%)
  starting transfers between devices  14.3 us (4%)
  between operations  13.5 us (4%)
    pallas_call x7, Pallas kernels, project(): pl.pallas_call(functools.partial(project_kernel, sub), grid=(span // tile...  180 us
    ppermute x15, waiting for transfers between devices, swap(): return lax.ppermute(value, axis, [(i, i ^ mask) for i in range(size)])  87.1 us
    ppermute x15, starting transfers between devices, swap(): return lax.ppermute(value, axis, [(i, i ^ mask) for i in range(size)])  14.2 us
    slice x4, local copies, waits for them, and re-layouts, on_device(): far_gates = [swap(gate_pre[:, s:s + n], 'dp', n_dp, far) for s, n in chunks]  11.9 us
    pallas_call x1, Pallas kernels, split_blocks(): pl.pallas_call(split_kernel, grid=(4,), in_specs=[pl.BlockSpec((step, n,...  7.11 us
  transfers between devices with their start and end apart: 18, of which 7 were waited for; matrix products, arithmetic and copies ran while one was open for 6% of the time, Pallas kernels for 53%

profile of v2, /device:TPU:0, one launch (start us, length us, event | category | flops | bytes accessed | tf_op | source)
XLA Modules:
  0.0 332.8 jit_solution(15701104533398445160)
XLA Ops:
  6.5 0.5 collective-permute-start.5
  7.0 7.1 %split_blocks.1 = bf16[4,512,512]{2,1,0:T(8,128)(2,1)} custom-call(bf16[512,4,512]{2,1,0:T(4,128)(2,1)} %grad_ref.1), custom_call_target="tpu_custom_call" | custom-call | tf_op jit(solution)/shard_map/split_blocks/pallas_call | solution.py:35
  14.1 2.3 fusion.1
  16.4 0.0 all-gather.7.cloned.1.call-update
  16.4 0.0 all-gather.11.cloned.1.call-start
  16.5 1.3 slice.34
  17.8 2.5 collective-permute-start.6
  20.3 23.7 %collective-permute-done.6 = bf16[2,512,512]{2,1,0:T(8,128)(2,1)S(1)} collective-permute-done((bf16[2,512,512]{2,1,0:T(8,128)(2,1)S(1)}, bf16[2,512,512]{2,1,0:T(8,128)(2,1)S(1)}, u32[]{:S(2)}, u32[]{:S(2)}) %collective-permute-start.6) | collective-permute-done | bytes 1048608 | tf_op jit(solution)/shard_map/ppermute | solution.py:17
  44.0 1.0 copy-done.12
  45.0 0.0 all-gather.11.cloned.1.call-update
  45.0 0.0 copy-start.15
  45.0 0.0 all-gather.9.cloned.1.call-start
  45.1 4.9 %fusion = (bf16[512,2048]{1,0:T(8,128)(2,1)}, bf16[512,2048]{1,0:T(8,128)(2,1)}) fusion(bf16[512,7168]{1,0:T(8,128)(2,1)} %gate_ref.3), kind=kLoop, calls=%fused_computation.7 | loop fusion | bytes 8388608 | tf_op jit(solution)/shard_map/slice | solution.py:152
  50.0 1.7 collective-permute-start.10
  51.7 0.7 fusion.2
  52.4 1.6 collective-permute-start.3
  54.0 0.0 collective-permute-start
  54.0 0.5 collective-permute-start.1
  54.6 0.0 all-gather.9.cloned.1.call-update
  54.6 2.7 slice.28
  57.3 2.4 slice.27
  59.7 1.9 slice.31
  61.6 1.6 copy.31.proj_ref
  63.3 5.3 %collective-permute-done.3 = f32[512,64]{1,0:T(8,128)S(1)} collective-permute-done((f32[512,64]{1,0:T(8,128)S(1)}, f32[512,64]{1,0:T(8,128)S(1)}, u32[]{:S(2)}, u32[]{:S(2)}) %collective-permute-start.3) | collective-permute-done | bytes 131104 | tf_op jit(solution)/shard_map/ppermute | solution.py:17
  68.6 1.5 collective-permute-start.9
  70.1 0.5 collective-permute-start.4
  70.6 30.9 %collective-permute-done.1 = bf16[64,1024]{1,0:T(8,128)(2,1)S(1)} collective-permute-done((bf16[64,1024]{1,0:T(8,128)(2,1)S(1)}, bf16[64,1024]{1,0:T(8,128)(2,1)S(1)}, u32[]{:S(2)}, u32[]{:S(2)}) %collective-permute-start.1) | collective-permute-done | bytes 131104 | tf_op jit(solution)/shard_map/ppermute | solution.py:17
  101.5 0.0 collective-permute-done.4
  101.6 1.8 collective-permute-start.8
  103.4 0.7 add.44.refs_0_
  104.1 0.0 collective-permute-done.2
  104.1 0.5 collective-permute-start.7
  104.6 0.0 collective-permute-done.5.near_ref
  104.7 1.6 collective-permute-start.11
  106.2 41.8 %project.7.refs_0_ = f32[256,64]{1,0:T(8,128)} custom-call(bf16[4,2,256,512]{3,2,1,0:T(8,128)(2,1)} %bitcast.14, bf16[512,7168]{1,0:T(8,128)(2,1)} %gate_ref.3, bf16[7168,2048]{1,0:T(8,128)(2,1)} %own_ref.13, bf16[7168,2048]{1,0:T(8,128)(2,1)} %collective-permute-done.5.near_ref, bf16[7168,64]{1,0:T(8,128)(2,1)} %copy.31.proj_ref, f32[512,64]{1,0:T(8,128)} %add.44.refs_0_), custom_call_target="tpu_custom_call" | custom-call | flops 15971909632 | bytes 62390272 | tf_op jit(solution)/shard_map/project/pallas_call | solution.py:95
  148.1 0.0 collective-permute-done.10.gate_ref
  148.1 4.4 %all-gather.11.cloned.1.call-done = bf16[8,512,512]{2,1,0:T(8,128)(2,1)} async-done(((bf16[2,512,512]{2,1,0:T(8,128)(2,1)}), bf16[8,512,512]{2,1,0:T(8,128)(2,1)}) %all-gather.11.cloned.1.call-update) | async-done | bytes 4194320 | tf_op jit(solution)/shard_map/all_gather | solution.py:146
  152.5 25.2 %project.8.refs_0_ = f32[512,64]{1,0:T(8,128)} custom-call(bf16[4,2,512,512]{3,2,1,0:T(8,128)(2,1)} %bitcast.8, bf16[512,2048]{1,0:T(8,128)(2,1)} %collective-permute-done.10.gate_ref, bf16[7168,2048]{1,0:T(8,128)(2,1)} %own_ref.13, bf16[7168,2048]{1,0:T(8,128)(2,1)} %collective-permute-done.5.near_ref, bf16[7168,64]{1,0:T(8,128)(2,1)} %copy.31.proj_ref, ...), custom_call_target="tpu_custom_call" | custom-call | flops 9126805504 | bytes 18874368 | tf_op jit(solution)/shard_map/project/pallas_call | solution.py:95
  177.7 0.0 collective-permute-done.9.gate_ref
  177.7 1.3 copy-done.9
  179.0 25.3 %project.9.refs_0_ = f32[512,64]{1,0:T(8,128)} custom-call(bf16[4,2,512,512]{3,2,1,0:T(8,128)(2,1)} %bitcast.9, bf16[512,2048]{1,0:T(8,128)(2,1)} %copy-done.9, bf16[7168,2048]{1,0:T(8,128)(2,1)} %own_ref.13, bf16[7168,2048]{1,0:T(8,128)(2,1)} %collective-permute-done.5.near_ref, bf16[7168,64]{1,0:T(8,128)(2,1)} %copy.31.proj_ref, f32[512,64]{1,0:T(8,128)} %project.8.refs_0_), custom_call_target="tpu_custom_call" | custom-call | flops 9126805504 | bytes 18874368 | tf_op jit(solution)/shard_map/project/pallas_call | solution.py:95
  204.3 0.0 collective-permute-done.8.gate_ref
  204.3 20.3 %project.10.refs_0_ = f32[512,64]{1,0:T(8,128)} custom-call(bf16[4,2,512,512]{3,2,1,0:T(8,128)(2,1)} %bitcast.10, bf16[512,1536]{1,0:T(8,128)(2,1)} %collective-permute-done.8.gate_ref, bf16[7168,2048]{1,0:T(8,128)(2,1)} %own_ref.13, bf16[7168,2048]{1,0:T(8,128)(2,1)} %collective-permute-done.5.near_ref, bf16[7168,64]{1,0:T(8,128)(2,1)} %copy.31.proj_ref, ...), custom_call_target="tpu_custom_call" | custom-call | flops 6845104128 | bytes 14155776 | tf_op jit(solution)/shard_map/project/pallas_call | solution.py:95
  224.6 0.0 collective-permute-done.7.gate_ref
  224.6 15.8 %project.11.refs_0_ = f32[512,64]{1,0:T(8,128)} custom-call(bf16[4,2,512,512]{3,2,1,0:T(8,128)(2,1)} %bitcast.11, bf16[512,1024]{1,0:T(8,128)(2,1)} %collective-permute-done.7.gate_ref, bf16[7168,2048]{1,0:T(8,128)(2,1)} %own_ref.13, bf16[7168,2048]{1,0:T(8,128)(2,1)} %collective-permute-done.5.near_ref, bf16[7168,64]{1,0:T(8,128)(2,1)} %copy.31.proj_ref, ...), custom_call_target="tpu_custom_call" | custom-call | flops 4563402752 | bytes 9437184 | tf_op jit(solution)/shard_map/project/pallas_call | solution.py:95
  240.4 0.0 all-gather.9.cloned.1.call-done
  240.4 41.8 %project.12.refs_0_ = f32[256,64]{1,0:T(8,128)} custom-call(bf16[4,2,256,512]{3,2,1,0:T(8,128)(2,1)} %bitcast.15, bf16[512,7168]{1,0:T(8,128)(2,1)} %gate_ref.3, bf16[7168,2048]{1,0:T(8,128)(2,1)} %own_ref.13, bf16[7168,2048]{1,0:T(8,128)(2,1)} %collective-permute-done.5.near_ref, bf16[7168,64]{1,0:T(8,128)(2,1)} %copy.31.proj_ref, f32[512,64]{1,0:T(8,128)} %project.11.refs_0_), custom_call_target="tpu_custom_call" | custom-call | flops 15971909632 | bytes 62390272 | tf_op jit(solution)/shard_map/project/pallas_call | solution.py:95
  282.2 0.0 copy-start.10
  282.3 0.0 collective-permute-done.11.gate_ref
  282.3 0.8 copy-done.14
  283.1 10.1 %project.13 = f32[512,64]{1,0:T(8,128)} custom-call(bf16[4,2,512,512]{3,2,1,0:T(8,128)(2,1)} %bitcast.12, bf16[512,512]{1,0:T(8,128)(2,1)} %copy-done.14, bf16[7168,2048]{1,0:T(8,128)(2,1)} %own_ref.13, bf16[7168,2048]{1,0:T(8,128)(2,1)} %collective-permute-done.5.near_ref, bf16[7168,64]{1,0:T(8,128)(2,1)} %copy.31.proj_ref, f32[256,64]{1,0:T(8,128)} %project.12.refs_0_), custom_call_target="tpu_custom_call" | custom-call | flops 2281701376 | bytes 4718592 | tf_op jit(solution)/shard_map/project/pallas_call | solution.py:95
  293.2 1.1 add_add_fusion
  294.3 0.8 collective-permute-start.12
  295.1 7.5 %collective-permute-done.12 = f32[512,64]{1,0:T(8,128)S(1)} collective-permute-done((f32[512,64]{1,0:T(8,128)S(1)}, f32[512,64]{1,0:T(8,128)S(1)}, u32[]{:S(2)}, u32[]{:S(2)}) %collective-permute-start.12) | collective-permute-done | bytes 131104 | tf_op jit(solution)/shard_map/ppermute | solution.py:17
  302.6 0.1 collective-permute-start.13
  302.7 7.4 %collective-permute-done.13 = f32[512,64]{1,0:T(8,128)S(1)} collective-permute-done((f32[512,64]{1,0:T(8,128)S(1)}, f32[512,64]{1,0:T(8,128)S(1)}, u32[]{:S(2)}, u32[]{:S(2)}) %collective-permute-start.13) | collective-permute-done | bytes 131104 | tf_op jit(solution)/shard_map/ppermute | solution.py:17
  310.1 0.5 collective-permute-start.14
  310.6 0.1 copy.30
  310.7 12.4 %collective-permute-done.14 = f32[512,64]{1,0:T(8,128)S(1)} collective-permute-done((f32[512,64]{1,0:T(8,128)S(1)}, f32[512,64]{1,0:T(8,128)S(1)}, u32[]{:S(2)}, u32[]{:S(2)}) %collective-permute-start.14) | collective-permute-done | bytes 131104 | tf_op jit(solution)/shard_map/ppermute | solution.py:17
  323.1 0.1 copy.38
  323.3 1.4 multiply_convert_fusion
  324.7 0.0 copy-start.1
  324.7 1.5 fusion.3
  326.2 0.1 copy-done.1
  (40 shorter events, 0.3 us)
Async XLA Ops:
  6.5 45.2 %copy-start = (bf16[512,2048]{1,0:T(8,128)(2,1)S(1)}, bf16[512,2048]{1,0:T(8,128)(2,1)}, u32[]{:S(2)}) copy-start(bf16[512,2048]{1,0:T(8,128)(2,1)} %param.7) | copy-start | bytes 6291460
  6.5 99.7 %all-gather.7.cloned.1.call-start = ((), (), s32[]{:S(2)}) async-start(), calls=%async_computation | async-start | bytes 2621440 | tf_op jit(solution)/shard_map/all_gather | solution.py:146
  6.5 98.1 %collective-permute-start.5 = (bf16[7168,2048]{1,0:T(8,128)(2,1)}, bf16[7168,2048]{1,0:T(8,128)(2,1)}, u32[]{:S(2)}, u32[]{:S(2)}) collective-permute-start(bf16[7168,2048]{1,0:T(8,128)(2,1)} %own_ref.13), channel_id=1, source_target_pairs={{0,1},{1,0},{2,3},{3,2},{4,5},{5,4},{6,7},{7,6},{8,9},{9,8},{10,11... | collective-permute-start | bytes 88080392 | tf_op jit(solution)/shard_map/ppermute | solution.py:17
  16.4 136.1 %all-gather.11.cloned.1.call-start = ((), (), s32[]{:S(2)}) async-start(), calls=%async_computation.2 | async-start | bytes 5242880 | tf_op jit(solution)/shard_map/all_gather | solution.py:146
  17.8 26.2 %collective-permute-start.6 = (bf16[2,512,512]{2,1,0:T(8,128)(2,1)S(1)}, bf16[2,512,512]{2,1,0:T(8,128)(2,1)S(1)}, u32[]{:S(2)}, u32[]{:S(2)}) collective-permute-start(bf16[2,512,512]{2,1,0:T(8,128)(2,1)S(1)} %slice.34), channel_id=1, source_target_pairs={{0,2},{1,3},{2,0},{3,1},{4,6},{5,7},{6,4},{7,5},{8,10},{9,11},{10,... | collective-permute-start | bytes 3145736 | tf_op jit(solution)/shard_map/ppermute | solution.py:17
  44.0 1.0 copy-start.12
  45.0 6.7 %copy-start.15 = (bf16[2048,64]{0,1:T(8,128)(2,1)S(1)}, bf16[2048,64]{0,1:T(8,128)(2,1)}, u32[]{:S(2)}) copy-start(bf16[2048,64]{0,1:T(8,128)(2,1)} %param.11) | copy-start | bytes 786436
  45.0 195.4 %all-gather.9.cloned.1.call-start = ((), (), s32[]{:S(2)}) async-start(), calls=%async_computation.1 | async-start | bytes 2621440 | tf_op jit(solution)/shard_map/all_gather | solution.py:146
  50.0 4.1 %copy-start.16 = (bf16[64,1024]{1,0:T(8,128)(2,1)S(1)}, bf16[64,1024]{1,0:T(8,128)(2,1)}, u32[]{:S(2)}) copy-start(bf16[64,1024]{1,0:T(8,128)(2,1)} %param.13) | copy-start | bytes 393220
  50.0 98.1 %collective-permute-start.10 = (bf16[512,2048]{1,0:T(8,128)(2,1)}, bf16[512,2048]{1,0:T(8,128)(2,1)}, u32[]{:S(2)}, u32[]{:S(2)}) collective-permute-start(bf16[512,2048]{1,0:T(8,128)(2,1)} %get-tuple-element.5), channel_id=1, source_target_pairs={{0,2},{1,3},{2,0},{3,1},{4,6},{5,7},{6,4},{7,5},{8,10},{9,11},{10,... | collective-permute-start | bytes 6291464 | tf_op jit(solution)/shard_map/ppermute | solution.py:17
  52.4 16.1 %collective-permute-start.3 = (f32[512,64]{1,0:T(8,128)S(1)}, f32[512,64]{1,0:T(8,128)S(1)}, u32[]{:S(2)}, u32[]{:S(2)}) collective-permute-start(f32[512,64]{1,0:T(8,128)S(1)} %fusion.2), channel_id=1, source_target_pairs={{0,4},{4,0},{8,12},{12,8},{1,5},{5,1},{9,13},{13,9},{2,6},{6,2},{1... | collective-permute-start | bytes 393224 | tf_op jit(solution)/shard_map/ppermute | solution.py:17
  54.0 16.0 %collective-permute-start = (bf16[64,1024]{1,0:T(8,128)(2,1)S(1)}, bf16[64,1024]{1,0:T(8,128)(2,1)S(1)}, u32[]{:S(2)}, u32[]{:S(2)}) collective-permute-start(bf16[64,1024]{1,0:T(8,128)(2,1)S(1)} %copy-done.16), channel_id=1, source_target_pairs={{0,1},{1,0},{2,3},{3,2},{4,5},{5,4},{6,7},{7,6},{8,9},{9,8},{10,11... | collective-permute-start | bytes 393224 | tf_op jit(solution)/shard_map/ppermute | solution.py:17
  54.0 47.5 %collective-permute-start.1 = (bf16[64,1024]{1,0:T(8,128)(2,1)S(1)}, bf16[64,1024]{1,0:T(8,128)(2,1)S(1)}, u32[]{:S(2)}, u32[]{:S(2)}) collective-permute-start(bf16[64,1024]{1,0:T(8,128)(2,1)S(1)} %copy-done.16), channel_id=1, source_target_pairs={{0,2},{1,3},{2,0},{3,1},{4,6},{5,7},{6,4},{7,5},{8,10},{9,11},{10,... | collective-permute-start | bytes 393224 | tf_op jit(solution)/shard_map/ppermute | solution.py:17
  57.3 4.3 %copy-start.13 = (bf16[7168,64]{0,1:T(8,128)(2,1)S(1)}, bf16[7168,64]{0,1:T(8,128)(2,1)}, u32[]{:S(2)}) copy-start(bf16[7168,64]{0,1:T(8,128)(2,1)} %param.12) | copy-start | bytes 2752516
  68.6 109.1 %collective-permute-start.9 = (bf16[512,2048]{1,0:T(8,128)(2,1)}, bf16[512,2048]{1,0:T(8,128)(2,1)S(1)}, u32[]{:S(2)}, u32[]{:S(2)}) collective-permute-start(bf16[512,2048]{1,0:T(8,128)(2,1)} %get-tuple-element.6), channel_id=1, source_target_pairs={{0,2},{1,3},{2,0},{3,1},{4,6},{5,7},{6,4},{7,5},{8,10},{9,11},{10,... | collective-permute-start | bytes 6291464 | tf_op jit(solution)/shard_map/ppermute | solution.py:17
  70.1 31.5 %collective-permute-start.4 = (f32[512,64]{1,0:T(8,128)S(1)}, f32[512,64]{1,0:T(8,128)S(1)}, u32[]{:S(2)}, u32[]{:S(2)}) collective-permute-start(f32[512,64]{1,0:T(8,128)S(1)} %add.43), channel_id=1, source_target_pairs={{0,8},{4,12},{8,0},{12,4},{1,9},{5,13},{9,1},{13,5},{2,10},{6,14},... | collective-permute-start | bytes 393224 | tf_op jit(solution)/shard_map/ppermute | solution.py:17
  101.5 2.6 collective-permute-start.2
  101.6 102.7 %collective-permute-start.8 = (bf16[512,1536]{1,0:T(8,128)(2,1)}, bf16[512,1536]{1,0:T(8,128)(2,1)}, u32[]{:S(2)}, u32[]{:S(2)}) collective-permute-start(bf16[512,1536]{1,0:T(8,128)(2,1)} %slice.28), channel_id=1, source_target_pairs={{0,2},{1,3},{2,0},{3,1},{4,6},{5,7},{6,4},{7,5},{8,10},{9,11},{10,... | collective-permute-start | bytes 4718600 | tf_op jit(solution)/shard_map/ppermute | solution.py:17
  104.1 120.5 %collective-permute-start.7 = (bf16[512,1024]{1,0:T(8,128)(2,1)}, bf16[512,1024]{1,0:T(8,128)(2,1)}, u32[]{:S(2)}, u32[]{:S(2)}) collective-permute-start(bf16[512,1024]{1,0:T(8,128)(2,1)} %slice.27), channel_id=1, source_target_pairs={{0,2},{1,3},{2,0},{3,1},{4,6},{5,7},{6,4},{7,5},{8,10},{9,11},{10,... | collective-permute-start | bytes 3145736 | tf_op jit(solution)/shard_map/ppermute | solution.py:17
  104.6 43.4 %copy-start.2 = (bf16[64,4096]{1,0:T(8,128)(2,1)}, bf16[64,4096]{1,0:T(8,128)(2,1)S(1)}, u32[]{:S(2)}) copy-start(bf16[64,4096]{1,0:T(8,128)(2,1)S(1)} %constant_dynamic-update-slice_fusion.refs_1_) | copy-start | bytes 1572868
  104.7 177.6 %collective-permute-start.11 = (bf16[512,512]{1,0:T(8,128)(2,1)}, bf16[512,512]{1,0:T(8,128)(2,1)S(1)}, u32[]{:S(2)}, u32[]{:S(2)}) collective-permute-start(bf16[512,512]{1,0:T(8,128)(2,1)} %slice.31), channel_id=1, source_target_pairs={{0,2},{1,3},{2,0},{3,1},{4,6},{5,7},{6,4},{7,5},{8,10},{9,11},{10,... | collective-permute-start | bytes 1572872 | tf_op jit(solution)/shard_map/ppermute | solution.py:17
  177.7 1.3 copy-start.9
  282.2 11.0 %copy-start.4 = (f32[512,64]{1,0:T(8,128)S(1)}, f32[512,64]{1,0:T(8,128)}, u32[]{:S(2)}) copy-start(f32[512,64]{1,0:T(8,128)} %project.8.refs_0_) | copy-start | bytes 393220
  282.2 11.0 %copy-start.5 = (f32[512,64]{1,0:T(8,128)S(1)}, f32[512,64]{1,0:T(8,128)}, u32[]{:S(2)}) copy-start(f32[512,64]{1,0:T(8,128)} %project.9.refs_0_) | copy-start | bytes 393220
  282.2 11.0 %copy-start.6 = (f32[512,64]{1,0:T(8,128)S(1)}, f32[512,64]{1,0:T(8,128)}, u32[]{:S(2)}) copy-start(f32[512,64]{1,0:T(8,128)} %project.10.refs_0_) | copy-start | bytes 393220
  282.2 11.0 %copy-start.7 = (f32[512,64]{1,0:T(8,128)S(1)}, f32[512,64]{1,0:T(8,128)}, u32[]{:S(2)}) copy-start(f32[512,64]{1,0:T(8,128)} %project.11.refs_0_) | copy-start | bytes 393220
  282.2 20.3 %copy-start.10 = (f32[256,64]{1,0:T(8,128)S(1)}, f32[256,64]{1,0:T(8,128)}, u32[]{:S(2)}) copy-start(f32[256,64]{1,0:T(8,128)} %project.7.refs_0_) | copy-start | bytes 196612
  282.3 20.3 %copy-start.11 = (f32[256,64]{1,0:T(8,128)S(1)}, f32[256,64]{1,0:T(8,128)}, u32[]{:S(2)}) copy-start(f32[256,64]{1,0:T(8,128)} %project.12.refs_0_) | copy-start | bytes 196612
  282.3 0.8 copy-start.14
  293.2 17.4 %copy-start.8 = (f32[512,64]{1,0:T(8,128)S(1)}, f32[512,64]{1,0:T(8,128)}, u32[]{:S(2)}) copy-start(f32[512,64]{1,0:T(8,128)} %add.44.refs_0_) | copy-start | bytes 393220
  294.3 8.3 %collective-permute-start.12 = (f32[512,64]{1,0:T(8,128)S(1)}, f32[512,64]{1,0:T(8,128)S(1)}, u32[]{:S(2)}, u32[]{:S(2)}) collective-permute-start(f32[512,64]{1,0:T(8,128)S(1)} %add_add_fusion), channel_id=1, source_target_pairs={{0,2},{1,3},{2,0},{3,1},{4,6},{5,7},{6,4},{7,5},{8,10},{9,11},{10,... | collective-permute-start | bytes 393224 | tf_op jit(solution)/shard_map/ppermute | solution.py:17
  302.6 7.4 %collective-permute-start.13 = (f32[512,64]{1,0:T(8,128)S(1)}, f32[512,64]{1,0:T(8,128)S(1)}, u32[]{:S(2)}, u32[]{:S(2)}) collective-permute-start(f32[512,64]{1,0:T(8,128)S(1)} %maximum_add_fusion), channel_id=1, source_target_pairs={{0,4},{4,0},{8,12},{12,8},{1,5},{5,1},{9,13},{13,9},{2,6},{6,2},{1... | collective-permute-start | bytes 393224 | tf_op jit(solution)/shard_map/ppermute | solution.py:17
  310.1 13.0 %collective-permute-start.14 = (f32[512,64]{1,0:T(8,128)S(1)}, f32[512,64]{1,0:T(8,128)S(1)}, u32[]{:S(2)}, u32[]{:S(2)}) collective-permute-start(f32[512,64]{1,0:T(8,128)S(1)} %add.50), channel_id=1, source_target_pairs={{0,8},{4,12},{8,0},{12,4},{1,9},{5,13},{9,1},{13,5},{2,10},{6,14},... | collective-permute-start | bytes 393224 | tf_op jit(solution)/shard_map/ppermute | solution.py:17
  323.3 1.4 copy-start.3
  324.7 1.6 copy-start.1
Sparse Core Ops, SparseCore 0:
  16.5 50.2 all-gather.6
  68.4 84.0 all-gather.10
  154.1 44.2 all-gather.8

commit v3 on v0

v3 whole, which is shorter than its diff:
```python
import functools

import jax
import jax.numpy as jnp
from jax import lax
from jax.experimental import pallas as pl
from jax.experimental.pallas import tpu as pltpu
from jax.sharding import PartitionSpec as P

LANES = 128
TILE = 512
RING = 4
VMEM = 60 * 1024 * 1024
ANY = pl.BlockSpec(memory_space=pl.ANY)


def swap(value, axis, size, mask):
    return lax.ppermute(value, axis, [(i, i ^ mask) for i in range(size)])


def split_kernel(grad_ref, *refs):
    me = lax.axis_index("dp")
    own_ref, far_ref = refs[-2:]
    blocks = [grad_ref[:, k, :] for k in range(grad_ref.shape[1])]
    bit = 1
    while bit < len(blocks):
        flip = (me & bit) != 0
        blocks = [jnp.where(flip, blocks[k ^ bit], blocks[k]) for k in range(len(blocks))]
        bit *= 2
    half = len(blocks) // 2
    for k in range(half):
        own_ref[k] = blocks[k]
        far_ref[k] = blocks[half + k]


def split_blocks(out_grad, after):
    rows, n, width = out_grad.shape
    step = rows // 4
    out = jax.ShapeDtypeStruct((n // 2, rows, width), out_grad.dtype)
    return pl.pallas_call(
        split_kernel,
        grid=(4,),
        in_specs=[pl.BlockSpec((step, n, width), lambda i: (i, 0, 0))] + [ANY] * len(after),
        out_specs=[pl.BlockSpec((n // 2, step, width), lambda i: (0, i, 0))] * 2,
        out_shape=[out, out],
        compiler_params=pltpu.CompilerParams(vmem_limit_bytes=VMEM),
        name="split_blocks",
    )(out_grad, *after)


def project_kernel(tiles, pieces, chained, *refs):
    grads = refs[:pieces]
    gate_ref, own_ref, near_ref, proj_ref = refs[pieces : pieces + 4]
    before_ref = refs[pieces + 4] if chained else None
    out_ref, rows_ref, even_ref, odd_ref, sum_ref, sems = refs[-6:]
    step = pl.program_id(0)
    pair, _, width = grads[0].shape

    def fill():
        shard = lax.axis_index("tensor")
        copies = []
        for k, grad_ref in enumerate(grads):
            column = lax.rem(shard + pieces - k, pieces) * width if pieces > 1 else 0
            columns = pl.ds(pl.multiple_of(column, width), width) if pieces > 1 else slice(None)
            for p in range(pair):
                copies.append(
                    pltpu.make_async_copy(grad_ref.at[p], rows_ref.at[p, :, columns], sems.at[k, p])
                )
        for copy in copies:
            copy.start()
        sum_ref[...] = jnp.zeros_like(sum_ref)
        for copy in copies:
            copy.wait()

    def multiply(hidden_ref):
        hidden = None
        for p, weight_ref in enumerate((own_ref, near_ref)):
            term = lax.dot_general(
                rows_ref[p],
                weight_ref[...],
                (((1,), (1,)), ((), ())),
                preferred_element_type=jnp.float32,
            )
            hidden = term if hidden is None else hidden + term
        hidden_ref[...] = hidden

    def reduce(hidden_ref):
        gate = gate_ref[...].astype(jnp.float32)
        below = 1.0 + jnp.exp(-gate)
        inverse = pl.reciprocal(below, approx=True)
        inverse = inverse * (2.0 - below * inverse)
        up_grad = (hidden_ref[...] * (gate * inverse)).astype(jnp.bfloat16)
        sum_ref[...] += jnp.dot(up_grad, proj_ref[...], preferred_element_type=jnp.float32)

    @pl.when(step == 0)
    def _():
        fill()
        multiply(even_ref)

    @pl.when((step > 0) & (step < tiles) & (lax.rem(step, 2) == 1))
    def _():
        reduce(even_ref)
        multiply(odd_ref)

    @pl.when((step > 0) & (step < tiles) & (lax.rem(step, 2) == 0))
    def _():
        reduce(odd_ref)
        multiply(even_ref)

    @pl.when(step == tiles)
    def _():
        reduce(even_ref if tiles % 2 else odd_ref)
        total = sum_ref[...].T
        out_ref[...] = total + before_ref[...] if chained else total


def project(grads, gate, weights, proj, offset, span, gate_column, before, after):
    pieces = len(grads)
    pair, rows, width = grads[0].shape
    depth = weights[0].shape[1]
    k = proj.shape[1]
    tile = TILE if span % TILE == 0 else span
    tiles = span // tile
    first, gate_first = offset // tile, gate_column // tile
    now = lambda i: first + jnp.minimum(i, tiles - 1)
    last = lambda i: jnp.maximum(i - 1, 0)
    chained = before is not None
    total = pl.BlockSpec((k, rows), lambda i: (0, 0))
    return pl.pallas_call(
        functools.partial(project_kernel, tiles, pieces, chained),
        grid=(tiles + 1,),
        in_specs=[ANY] * pieces
        + [
            pl.BlockSpec((rows, tile), lambda i: (0, gate_first + last(i))),
            pl.BlockSpec((tile, depth), lambda i: (now(i), 0)),
            pl.BlockSpec((tile, depth), lambda i: (now(i), 0)),
            pl.BlockSpec((tile, k), lambda i: (first + last(i), 0)),
        ]
        + [total] * chained
        + [ANY] * len(after),
        out_specs=total,
        out_shape=jax.ShapeDtypeStruct((k, rows), jnp.float32),
        scratch_shapes=[
            pltpu.VMEM((pair, rows, depth), grads[0].dtype),
            pltpu.VMEM((rows, tile), jnp.float32),
            pltpu.VMEM((rows, tile), jnp.float32),
            pltpu.VMEM((rows, k), jnp.float32),
            pltpu.SemaphoreType.DMA((pieces, pair)),
        ],
        compiler_params=pltpu.CompilerParams(vmem_limit_bytes=VMEM),
        cost_estimate=pl.CostEstimate(
            flops=2 * rows * span * (pair * depth + 4 * k),
            bytes_accessed=2 * span * (pair * depth + rows),
            transcendentals=rows * span,
        ),
        name="project",
    )(*grads, gate, *weights, proj, *([before] if chained else []), *after)


def score_kernel(input_ref, grad_ref, other_ref, query_ref, out_ref):
    grad = grad_ref[...] + other_ref[...]
    high = grad.astype(jnp.bfloat16)
    low = (grad - high.astype(jnp.float32)).astype(jnp.bfloat16)
    both = jnp.concatenate([high, low], axis=0)
    total = jnp.zeros_like(out_ref)
    for i in range(query_ref.shape[0]):
        part = jnp.dot(query_ref[i], both, preferred_element_type=jnp.float32)
        total += input_ref[i : i + 1, :] * part
    out_ref[...] = total


def score(input_proj, grad, other, queries):
    k, rows = grad.shape
    count = queries.shape[0]
    pairs = queries.reshape(count, k, k).transpose(1, 0, 2)
    pairs = jnp.concatenate([pairs, pairs], axis=2)
    return pairs, lambda grad, other, pairs: pl.pallas_call(
        score_kernel,
        out_shape=jax.ShapeDtypeStruct((count, rows), jnp.float32),
        compiler_params=pltpu.CompilerParams(vmem_limit_bytes=VMEM),
        name="score",
    )(input_proj, grad, other, pairs)


def chunks_of(hidden):
    units = hidden // TILE
    if hidden % TILE or units < 8:
        return [(0, hidden)]
    cuts = [0, round(units / 7), units - 3, units - 1, units]
    return [(a * TILE, (b - a) * TILE) for a, b in zip(cuts, cuts[1:]) if b > a]


def on_device(n_dp, n_tensor, inputs, out_grad, gate_pre, down_weight, proj_in, proj_out, queries):
    rows = out_grad.shape[0]
    hidden = gate_pre.shape[1]
    me = lax.axis_index("dp")
    far, near = n_dp // 2, 1

    def gather(block, hold=None):
        if n_tensor > RING or block.shape[2] % LANES:
            grad = lax.all_gather(block, "tensor", axis=0, tiled=False)
            return [jnp.transpose(grad, (1, 2, 0, 3)).reshape(2, rows, -1)]
        pieces = [block]
        for k in range(n_tensor - 1):
            piece = pieces[-1]
            if k == 1 and hold is not None:
                piece, _ = lax.optimization_barrier((piece, hold))
                pieces[-1] = piece
            pieces.append(
                lax.ppermute(piece, "tensor", [(i, (i + 1) % n_tensor) for i in range(n_tensor)])
            )
        return pieces

    chunks = chunks_of(hidden)
    weights = (down_weight, swap(down_weight, "dp", n_dp, near))

    far_query = swap(queries, "dp", n_dp, far)
    near_query = swap(queries, "dp", n_dp, near)
    diag_query = swap(far_query, "dp", n_dp, near)

    def cut(source, chunk):
        return source[:, chunk[0] : chunk[0] + chunk[1]]

    first = cut(gate_pre, chunks[0])
    own_blocks, far_blocks = split_blocks(out_grad, (first,))
    later = [cut(gate_pre, chunk) for chunk in chunks[1:]]
    if later:
        later[0], far_blocks, _ = lax.optimization_barrier((later[0], far_blocks, far_query))
    far_gates = [swap(part, "dp", n_dp, far) for part in [first] + later]
    grads_own = gather(own_blocks, far_gates[0])
    grads_far = gather(swap(far_blocks, "dp", n_dp, far))

    input_proj = lax.dot_general(
        proj_in, inputs, (((0,), (1,)), ((), ())), preferred_element_type=jnp.float32
    )
    mask = 1
    while mask < n_tensor:
        input_proj = input_proj + swap(input_proj, "tensor", n_tensor, mask)
        mask *= 2

    width = queries.shape[1]
    all_queries = jnp.zeros((queries.shape[0], n_dp * width), queries.dtype)
    for mask, block in enumerate((queries, near_query, far_query, diag_query)):
        all_queries = lax.dynamic_update_slice(all_queries, block, (0, (me ^ mask) * width))
    pairs, finish = score(input_proj, input_proj, input_proj, all_queries)

    middle = hidden // 2 if hidden % (2 * TILE) == 0 else 0
    own_sum = None
    after = (input_proj, pairs)
    for s, n in ((0, middle), (middle, hidden - middle)):
        if n:
            own_sum = project(grads_own, gate_pre, weights, proj_out, s, n, s, own_sum, after)
            after = (own_sum,)
    far_sum = None
    for gate, (s, n) in zip(far_gates, chunks):
        far_sum = project(grads_far, gate, weights, proj_out, s, n, 0, far_sum, after)
        after = ()

    value = own_sum + swap(far_sum, "dp", n_dp, far)
    mask = 1
    while mask < n_tensor:
        other = swap(value, "tensor", n_tensor, mask)
        mask *= 2
        if mask < n_tensor:
            value = value + other
    return finish(value, other, pairs)


def solution(mesh):
    return jax.shard_map(
        functools.partial(on_device, mesh.shape["dp"], mesh.shape["tensor"]),
        mesh=mesh,
        in_specs=(
            P(("parts", "dp"), "tensor"),
            P(("parts", "dp"), None, "tensor"),
            P(("parts", "dp"), "tensor"),
            P("tensor", "dp"),
            P("tensor", None),
            P("tensor", None),
            P("tensor", "dp"),
        ),
        out_specs=P("tensor", ("parts", "dp")),
        check_vma=False,
    )
```

time: 962 us -> 302 us (0.31)
  waiting for transfers between devices: 841 us -> 132 us
  Pallas kernels: 0 us -> 127 us
  matrix products: 78 us -> 0.77 us
  starting transfers between devices: 0.08 us -> 15.6 us
  between operations: 13.2 us -> 0.48 us
    all_gather x2 -> x0, waiting for transfers between devices: 811 us -> none  [the longest x1 660 us: on_device(): lax.all_gather(down_weight, 'dp', axis=1, tiled=True)]
    ppermute x0 -> x20, waiting for transfers between devices: none -> 132 us  [the longest x14 77.5 us: swap(): return lax.ppermute(value, axis, [(i, i ^ mask) for i in range(size)])]
    pallas_call x0 -> x8, Pallas kernels: none -> 127 us  [the longest x6 116 us: project(): pl.pallas_call(functools.partial(project_kernel, tiles, pieces, chained),...]
    dot_general x4 -> x1, matrix products: 78 us -> 0.77 us  [on_device(): lax.dot_general(proj_in, inputs, (((0,), (1,)), ((), ())), preferred_elem...]
    psum x1 -> x0, waiting for transfers between devices: 28.5 us -> none  [on_device(): grad_proj = lax.psum(grad_part, 'tensor')]
    ppermute x0 -> x20, starting transfers between devices: none -> 15.6 us  [the longest x14 11.8 us: swap(): return lax.ppermute(value, axis, [(i, i ^ mask) for i in range(size)])]
    unnamed x9 -> x31, local copies, waits for them, and re-layouts: 19.6 us -> 6.68 us
    slice x0 -> x3, local copies, waits for them, and re-layouts: none -> 9.76 us  [cut(): return source[:, chunk[0]:chunk[0] + chunk[1]]]
  transfers between devices with their start and end apart: 3 -> 20, of which waited for: 3 -> 10; matrix products, arithmetic and copies ran while one was open for 2% -> 6% of each run, Pallas kernels for 0% -> 39%
where the time goes in v3:
time: 302 us; the launch traced here: 296 us
  waiting for transfers between devices  132 us (44%)
  Pallas kernels  127 us (42%)
  local copies, waits for them, and re-layouts  18.3 us (6%)
  starting transfers between devices  15.6 us (5%)
    pallas_call x6, Pallas kernels, project(): pl.pallas_call(functools.partial(project_kernel, tiles, pieces, chained),...  116 us
    ppermute x14, waiting for transfers between devices, swap(): return lax.ppermute(value, axis, [(i, i ^ mask) for i in range(size)])  77.5 us
    ppermute x6, waiting for transfers between devices, gather(): lax.ppermute(piece, 'tensor', [(i, (i + 1) % n_tensor) for i in range(n_t...  54.2 us
    ppermute x14, starting transfers between devices, swap(): return lax.ppermute(value, axis, [(i, i ^ mask) for i in range(size)])  11.8 us
    slice x3, local copies, waits for them, and re-layouts, cut(): return source[:, chunk[0]:chunk[0] + chunk[1]]  9.76 us
    pallas_call x1, Pallas kernels, split_blocks(): pl.pallas_call(split_kernel, grid=(4,), in_specs=[pl.BlockSpec((step, n,...  6.99 us
    unnamed x31, local copies, waits for them, and re-layouts  6.68 us
  transfers between devices with their start and end apart: 20, of which 10 were waited for; matrix products, arithmetic and copies ran while one was open for 6% of the time, Pallas kernels for 39%

profile of v3, /device:TPU:0, one launch (start us, length us, event | category | flops | bytes accessed | tf_op | source)
XLA Modules:
  0.0 296.2 jit_solution(15162136047774695874)
XLA Ops:
  0.0 0.5 collective-permute-start.6
  0.5 2.6 collective-permute-start.8
  3.0 3.1 %fusion = (bf16[512,1024]{1,0:T(8,128)(2,1)}, bf16[512,1024]{1,0:T(8,128)(2,1)}) fusion(bf16[512,7168]{1,0:T(8,128)(2,1)} %refs_4_.3), kind=kLoop, calls=%fused_computation.6 | loop fusion | bytes 4194304 | tf_op jit(solution)/shard_map/slice | solution.py:222
  6.1 0.2 collective-permute-start.3
  6.3 7.0 %split_blocks.1 = (bf16[2,512,512]{2,1,0:T(8,128)(2,1)}, bf16[2,512,512]{2,1,0:T(8,128)(2,1)}) custom-call(bf16[512,4,512]{2,1,0:T(4,128)(2,1)} %grad_ref.1, bf16[512,1024]{1,0:T(8,128)(2,1)} %get-tuple-element.16.refs_0_), custom_call_target="tpu_custom_call" | custom-call | tf_op jit(solution)/shard_map/split_blocks/pallas_call | solution.py:40
  13.3 2.0 collective-permute-start.2
  15.3 4.8 %slice.13 = bf16[512,4608]{1,0:T(8,128)(2,1)} slice(bf16[512,7168]{1,0:T(8,128)(2,1)} %refs_4_.3), slice={[0:512], [1024:5632]} | slice | bytes 9437184 | tf_op jit(solution)/shard_map/slice | solution.py:222
  20.1 0.0 collective-permute-done.8
  20.1 1.5 collective-permute-start.10
  21.5 19.2 %collective-permute-done.2.refs_1_ = bf16[2,512,512]{2,1,0:T(8,128)(2,1)S(1)} collective-permute-done((bf16[2,512,512]{2,1,0:T(8,128)(2,1)}, bf16[2,512,512]{2,1,0:T(8,128)(2,1)S(1)}, u32[]{:S(2)}, u32[]{:S(2)}) %collective-permute-start.2) | collective-permute-done | bytes 1048608 | tf_op jit(solution)/shard_map/ppermute | solution.py:210
  40.7 0.0 collective-permute-done.3.refs_4_
  40.7 0.0 collective-permute-start.4
  40.7 13.3 %collective-permute-done.10.refs_0_ = bf16[2,512,512]{2,1,0:T(8,128)(2,1)S(1)} collective-permute-done((bf16[2,512,512]{2,1,0:T(8,128)(2,1)S(1)}, bf16[2,512,512]{2,1,0:T(8,128)(2,1)S(1)}, u32[]{:S(2)}, u32[]{:S(2)}) %collective-permute-start.10) | collective-permute-done | bytes 1048608 | tf_op jit(solution)/shard_map/ppermute | solution.py:18
  54.0 1.6 collective-permute-start.11
  55.6 0.5 collective-permute-start.16
  56.1 12.6 %collective-permute-done.4.refs_2_ = bf16[2,512,512]{2,1,0:T(8,128)(2,1)} collective-permute-done((bf16[2,512,512]{2,1,0:T(8,128)(2,1)S(1)}, bf16[2,512,512]{2,1,0:T(8,128)(2,1)}, u32[]{:S(2)}, u32[]{:S(2)}) %collective-permute-start.4) | collective-permute-done | bytes 1048608 | tf_op jit(solution)/shard_map/ppermute | solution.py:210
  68.7 0.0 collective-permute-start.5
  68.7 22.5 %collective-permute-done.11.refs_1_ = bf16[2,512,512]{2,1,0:T(8,128)(2,1)} collective-permute-done((bf16[2,512,512]{2,1,0:T(8,128)(2,1)S(1)}, bf16[2,512,512]{2,1,0:T(8,128)(2,1)}, u32[]{:S(2)}, u32[]{:S(2)}) %collective-permute-start.11) | collective-permute-done | bytes 1048608 | tf_op jit(solution)/shard_map/ppermute | solution.py:210
  91.2 0.0 collective-permute-start.12
  91.2 0.0 copy-done.11
  91.2 0.1 collective-permute-start.7
  91.3 0.8 fusion.1
  92.1 0.5 collective-permute-done.7
  92.6 0.7 copy-done.12
  93.3 0.0 collective-permute-start
  93.3 43.8 %collective-permute-done = f32[64,512]{1,0:T(8,128)S(1)} collective-permute-done((f32[64,512]{1,0:T(8,128)S(1)}, f32[64,512]{1,0:T(8,128)S(1)}, u32[]{:S(2)}, u32[]{:S(2)}) %collective-permute-start) | collective-permute-done | bytes 131104 | tf_op jit(solution)/shard_map/ppermute | solution.py:18
  137.1 0.1 collective-permute-start.9
  137.3 0.0 copy-start.13
  137.3 1.9 slice.14
  139.2 2.6 copy.16.refs_7_
  141.9 0.0 collective-permute-done.9
  141.9 0.5 collective-permute-start.1
  142.4 1.1 reshape.3
  143.5 0.7 copy.22
  144.2 6.2 %collective-permute-done.1 = f32[64,512]{1,0:T(8,128)S(1)} collective-permute-done((f32[64,512]{1,0:T(8,128)S(1)}, f32[64,512]{1,0:T(8,128)S(1)}, u32[]{:S(2)}, u32[]{:S(2)}) %collective-permute-start.1) | collective-permute-done | bytes 131104 | tf_op jit(solution)/shard_map/ppermute | solution.py:18
  150.4 1.3 collective-permute-start.15
  151.7 0.7 add.25.refs_8_.input_ref
  152.4 1.6 pad_maximum_fusion.refs_9_.query_ref
  154.0 0.0 collective-permute-done.5.refs_3_
  154.0 0.7 collective-permute-start.14
  154.7 0.0 collective-permute-done.12.refs_2_
  154.7 0.2 collective-permute-start.13
  154.9 0.0 collective-permute-done.6.refs_6_
  154.9 25.6 %project.6.refs_8_.refs_9_ = f32[64,512]{1,0:T(8,128)} custom-call(bf16[2,512,512]{2,1,0:T(8,128)(2,1)} %get-tuple-element.10.refs_0_, bf16[2,512,512]{2,1,0:T(8,128)(2,1)} %copy-done.4, bf16[2,512,512]{2,1,0:T(8,128)(2,1)} %collective-permute-done.4.refs_2_, bf16[2,512,512]{2,1,0:T(8,128)(2,1)} %collective-permute-done.5.refs_3_, ...), custom_call_target="tpu_custom_call" | custom-call | flops 15971909632 | bytes 33030144 | tf_op jit(solution)/shard_map/project/pallas_call | solution.py:129
  180.5 26.2 %project.7.refs_8_ = f32[64,512]{1,0:T(8,128)} custom-call(bf16[2,512,512]{2,1,0:T(8,128)(2,1)} %get-tuple-element.10.refs_0_, bf16[2,512,512]{2,1,0:T(8,128)(2,1)} %copy-done.4, bf16[2,512,512]{2,1,0:T(8,128)(2,1)} %collective-permute-done.4.refs_2_, bf16[2,512,512]{2,1,0:T(8,128)(2,1)} %collective-permute-done.5.refs_3_, bf16[512,7168]{1,0:T(8,128)(2,1)} %refs_4_.3, ...), custom_call_target="tpu_custom_call" | custom-call | flops 15971909632 | bytes 33030144 | tf_op jit(solution)/shard_map/project/pallas_call | solution.py:129
  206.8 0.0 collective-permute-done.13.refs_3_
  206.8 1.0 copy-done.3
  207.8 11.8 %project.8.refs_8_ = f32[64,512]{1,0:T(8,128)} custom-call(bf16[2,512,512]{2,1,0:T(8,128)(2,1)} %copy-done.2, bf16[2,512,512]{2,1,0:T(8,128)(2,1)} %collective-permute-done.11.refs_1_, bf16[2,512,512]{2,1,0:T(8,128)(2,1)} %collective-permute-done.12.refs_2_, bf16[2,512,512]{2,1,0:T(8,128)(2,1)} %copy-done.3, ...), custom_call_target="tpu_custom_call" | custom-call | flops 4563402752 | bytes 9437184 | tf_op jit(solution)/shard_map/project/pallas_call | solution.py:129
  219.6 0.0 collective-permute-done.16.refs_4_
  219.6 31.9 %project.9.refs_8_ = f32[64,512]{1,0:T(8,128)} custom-call(bf16[2,512,512]{2,1,0:T(8,128)(2,1)} %copy-done.2, bf16[2,512,512]{2,1,0:T(8,128)(2,1)} %collective-permute-done.11.refs_1_, bf16[2,512,512]{2,1,0:T(8,128)(2,1)} %collective-permute-done.12.refs_2_, bf16[2,512,512]{2,1,0:T(8,128)(2,1)} %copy-done.3, ...), custom_call_target="tpu_custom_call" | custom-call | flops 20535312384 | bytes 42467328 | tf_op jit(solution)/shard_map/project/pallas_call | solution.py:129
  251.5 0.0 collective-permute-done.15.refs_4_
  251.5 1.0 copy-done.6
  252.5 12.4 %project.10.refs_8_ = f32[64,512]{1,0:T(8,128)} custom-call(bf16[2,512,512]{2,1,0:T(8,128)(2,1)} %copy-done.2, bf16[2,512,512]{2,1,0:T(8,128)(2,1)} %collective-permute-done.11.refs_1_, bf16[2,512,512]{2,1,0:T(8,128)(2,1)} %collective-permute-done.12.refs_2_, bf16[2,512,512]{2,1,0:T(8,128)(2,1)} %copy-done.3, bf16[512,1024]{1,0:T(8,128)(2,1)} %copy-done.6, ...), custom_call_target="tpu_custom_call" | custom-call | flops 4563402752 | bytes 9437184 | tf_op jit(solution)/shard_map/project/pallas_call | solution.py:129
  264.8 0.0 collective-permute-done.14.refs_4_
  264.9 0.8 copy-done.7
  265.7 8.6 %project.11 = f32[64,512]{1,0:T(8,128)} custom-call(bf16[2,512,512]{2,1,0:T(8,128)(2,1)} %copy-done.2, bf16[2,512,512]{2,1,0:T(8,128)(2,1)} %collective-permute-done.11.refs_1_, bf16[2,512,512]{2,1,0:T(8,128)(2,1)} %collective-permute-done.12.refs_2_, bf16[2,512,512]{2,1,0:T(8,128)(2,1)} %copy-done.3, bf16[512,512]{1,0:T(8,128)(2,1)} %copy-done.7, ...), custom_call_target="tpu_custom_call" | custom-call | flops 2281701376 | bytes 4718592 | tf_op jit(solution)/shard_map/project/pallas_call | solution.py:129
  274.3 1.3 collective-permute-start.17
  275.6 3.9 %collective-permute-done.17 = f32[64,512]{1,0:T(8,128)S(1)} collective-permute-done((f32[64,512]{1,0:T(8,128)}, f32[64,512]{1,0:T(8,128)S(1)}, u32[]{:S(2)}, u32[]{:S(2)}) %collective-permute-start.17) | collective-permute-done | bytes 131104 | tf_op jit(solution)/shard_map/ppermute | solution.py:18
  279.6 0.2 collective-permute-start.18
  279.7 4.9 %collective-permute-done.18 = f32[64,512]{1,0:T(8,128)S(1)} collective-permute-done((f32[64,512]{1,0:T(8,128)S(1)}, f32[64,512]{1,0:T(8,128)S(1)}, u32[]{:S(2)}, u32[]{:S(2)}) %collective-permute-start.18) | collective-permute-done | bytes 131104 | tf_op jit(solution)/shard_map/ppermute | solution.py:18
  284.6 2.5 collective-permute-start.19
  287.1 4.9 %collective-permute-done.19.other_ref = f32[64,512]{1,0:T(8,128)S(1)} collective-permute-done((f32[64,512]{1,0:T(8,128)S(1)}, f32[64,512]{1,0:T(8,128)S(1)}, u32[]{:S(2)}, u32[]{:S(2)}) %collective-permute-start.19) | collective-permute-done | bytes 131104 | tf_op jit(solution)/shard_map/ppermute | solution.py:18
  292.0 0.7 copy-done.10
  292.6 3.3 %score.1 = f32[64,512]{1,0:T(8,128)} custom-call(f32[64,512]{1,0:T(8,128)} %add.25.refs_8_.input_ref, f32[64,512]{1,0:T(8,128)} %copy-done.8, f32[64,512]{1,0:T(8,128)} %copy-done.10, bf16[64,64,128]{2,1,0:T(8,128)(2,1)} %pad_maximum_fusion.refs_9_.query_ref), custom_call_target="tpu_custom_call" | custom-call | tf_op jit(solution)/shard_map/score/pallas_call | solution.py:177
  (31 shorter events, 0.2 us)
Async XLA Ops:
  0.0 91.3 %copy-start = (bf16[512,2048]{1,0:T(8,128)(2,1)S(1)}, bf16[512,2048]{1,0:T(8,128)(2,1)}, u32[]{:S(2)}) copy-start(bf16[512,2048]{1,0:T(8,128)(2,1)} %param.7) | copy-start | bytes 6291460
  0.0 154.9 %collective-permute-start.6 = (bf16[7168,2048]{1,0:T(8,128)(2,1)}, bf16[7168,2048]{1,0:T(8,128)(2,1)}, u32[]{:S(2)}, u32[]{:S(2)}) collective-permute-start(bf16[7168,2048]{1,0:T(8,128)(2,1)} %refs_5_.11), channel_id=1, source_target_pairs={{0,1},{1,0},{2,3},{3,2},{4,5},{5,4},{6,7},{7,6},{8,9},{9,8},{10,11... | collective-permute-start | bytes 88080392 | tf_op jit(solution)/shard_map/ppermute | solution.py:18
  0.5 19.6 %collective-permute-start.8 = (bf16[64,1024]{1,0:T(8,128)(2,1)}, bf16[64,1024]{1,0:T(8,128)(2,1)S(1)}, u32[]{:S(2)}, u32[]{:S(2)}) collective-permute-start(bf16[64,1024]{1,0:T(8,128)(2,1)} %param.13), channel_id=1, source_target_pairs={{0,2},{1,3},{2,0},{3,1},{4,6},{5,7},{6,4},{7,5},{8,10},{9,11},{10,... | collective-permute-start | bytes 393224 | tf_op jit(solution)/shard_map/ppermute | solution.py:18
  6.1 34.6 %collective-permute-start.3 = (bf16[512,1024]{1,0:T(8,128)(2,1)}, bf16[512,1024]{1,0:T(8,128)(2,1)}, u32[]{:S(2)}, u32[]{:S(2)}) collective-permute-start(bf16[512,1024]{1,0:T(8,128)(2,1)} %get-tuple-element.16.refs_0_), channel_id=1, source_target_pairs={{0,2},{1,3},{2,0},{3,1},{4,6},{5,7},{6,4},{7,5},{8,10},{9,11},{10,... | collective-permute-start | bytes 3145736 | tf_op jit(solution)/shard_map/ppermute | solution.py:18
  13.2 6.8 %copy-start.14 = (bf16[2,512,512]{2,1,0:T(8,128)(2,1)S(1)}, bf16[2,512,512]{2,1,0:T(8,128)(2,1)}, u32[]{:S(2)}) copy-start(bf16[2,512,512]{2,1,0:T(8,128)(2,1)} %get-tuple-element.13) | copy-start | bytes 3145732
  13.2 77.9 %copy-start.11 = (bf16[64,1024]{1,0:T(8,128)(2,1)S(1)}, bf16[64,1024]{1,0:T(8,128)(2,1)}, u32[]{:S(2)}) copy-start(bf16[64,1024]{1,0:T(8,128)(2,1)} %param.13) | copy-start | bytes 393220
  13.2 78.0 %copy-start.9 = (bf16[2048,64]{0,1:T(8,128)(2,1)S(1)}, bf16[2048,64]{0,1:T(8,128)(2,1)}, u32[]{:S(2)}) copy-start(bf16[2048,64]{0,1:T(8,128)(2,1)} %param.11) | copy-start | bytes 786436
  13.3 27.5 %collective-permute-start.2 = (bf16[2,512,512]{2,1,0:T(8,128)(2,1)}, bf16[2,512,512]{2,1,0:T(8,128)(2,1)S(1)}, u32[]{:S(2)}, u32[]{:S(2)}) collective-permute-start(bf16[2,512,512]{2,1,0:T(8,128)(2,1)} %get-tuple-element.10.refs_0_), channel_id=1, source_target_pairs={{0,4},{4,8},{8,12},{12,0},{1,5},{5,9},{9,13},{13,1},{2,6},{6,10},{... | collective-permute-start | bytes 3145736 | tf_op jit(solution)/shard_map/ppermute | solution.py:210
  20.1 33.9 %collective-permute-start.10 = (bf16[2,512,512]{2,1,0:T(8,128)(2,1)S(1)}, bf16[2,512,512]{2,1,0:T(8,128)(2,1)S(1)}, u32[]{:S(2)}, u32[]{:S(2)}) collective-permute-start(bf16[2,512,512]{2,1,0:T(8,128)(2,1)S(1)} %copy-done.14), channel_id=1, source_target_pairs={{0,2},{1,3},{2,0},{3,1},{4,6},{5,7},{6,4},{7,5},{8,10},{9,11},{10,... | collective-permute-start | bytes 3145736 | tf_op jit(solution)/shard_map/ppermute | solution.py:18
  40.7 50.5 %copy-start.4 = (bf16[2,512,512]{2,1,0:T(8,128)(2,1)}, bf16[2,512,512]{2,1,0:T(8,128)(2,1)S(1)}, u32[]{:S(2)}) copy-start(bf16[2,512,512]{2,1,0:T(8,128)(2,1)S(1)} %collective-permute-done.2.refs_1_) | copy-start | bytes 3145732
  40.7 28.0 %collective-permute-start.4 = (bf16[2,512,512]{2,1,0:T(8,128)(2,1)S(1)}, bf16[2,512,512]{2,1,0:T(8,128)(2,1)}, u32[]{:S(2)}, u32[]{:S(2)}) collective-permute-start(bf16[2,512,512]{2,1,0:T(8,128)(2,1)S(1)} %collective-permute-done.2.refs_1_), channel_id=1, source_target_pairs={{0,4},{4,8},{8,12},{12,0},{1,5},{5,9},{9,13},{13,1},{2,6},{6,10},{... | collective-permute-start | bytes 3145736 | tf_op jit(solution)/shard_map/ppermute | solution.py:210
  54.0 85.2 %copy-start.2 = (bf16[2,512,512]{2,1,0:T(8,128)(2,1)}, bf16[2,512,512]{2,1,0:T(8,128)(2,1)S(1)}, u32[]{:S(2)}) copy-start(bf16[2,512,512]{2,1,0:T(8,128)(2,1)S(1)} %collective-permute-done.10.refs_0_) | copy-start | bytes 3145732
  54.0 37.2 %collective-permute-start.11 = (bf16[2,512,512]{2,1,0:T(8,128)(2,1)S(1)}, bf16[2,512,512]{2,1,0:T(8,128)(2,1)}, u32[]{:S(2)}, u32[]{:S(2)}) collective-permute-start(bf16[2,512,512]{2,1,0:T(8,128)(2,1)S(1)} %collective-permute-done.10.refs_0_), channel_id=1, source_target_pairs={{0,4},{4,8},{8,12},{12,0},{1,5},{5,9},{9,13},{13,1},{2,6},{6,10},{... | collective-permute-start | bytes 3145736 | tf_op jit(solution)/shard_map/ppermute | solution.py:210
  55.6 164.0 %collective-permute-start.16 = (bf16[512,4608]{1,0:T(8,128)(2,1)}, bf16[512,4608]{1,0:T(8,128)(2,1)}, u32[]{:S(2)}, u32[]{:S(2)}) collective-permute-start(bf16[512,4608]{1,0:T(8,128)(2,1)} %slice.13), channel_id=1, source_target_pairs={{0,2},{1,3},{2,0},{3,1},{4,6},{5,7},{6,4},{7,5},{8,10},{9,11},{10,... | collective-permute-start | bytes 14155784 | tf_op jit(solution)/shard_map/ppermute | solution.py:18
  68.7 85.3 %collective-permute-start.5 = (bf16[2,512,512]{2,1,0:T(8,128)(2,1)}, bf16[2,512,512]{2,1,0:T(8,128)(2,1)}, u32[]{:S(2)}, u32[]{:S(2)}) collective-permute-start(bf16[2,512,512]{2,1,0:T(8,128)(2,1)} %collective-permute-done.4.refs_2_), channel_id=1, source_target_pairs={{0,4},{4,8},{8,12},{12,0},{1,5},{5,9},{9,13},{13,1},{2,6},{6,10},{... | collective-permute-start | bytes 3145736 | tf_op jit(solution)/shard_map/ppermute | solution.py:210
  91.2 63.6 %collective-permute-start.12 = (bf16[2,512,512]{2,1,0:T(8,128)(2,1)}, bf16[2,512,512]{2,1,0:T(8,128)(2,1)}, u32[]{:S(2)}, u32[]{:S(2)}) collective-permute-start(bf16[2,512,512]{2,1,0:T(8,128)(2,1)} %collective-permute-done.11.refs_1_), channel_id=1, source_target_pairs={{0,4},{4,8},{8,12},{12,0},{1,5},{5,9},{9,13},{13,1},{2,6},{6,10},{... | collective-permute-start | bytes 3145736 | tf_op jit(solution)/shard_map/ppermute | solution.py:210
  91.2 1.4 collective-permute-start.7
  92.6 0.7 copy-start.12
  93.3 43.8 %collective-permute-start = (f32[64,512]{1,0:T(8,128)S(1)}, f32[64,512]{1,0:T(8,128)S(1)}, u32[]{:S(2)}, u32[]{:S(2)}) collective-permute-start(f32[64,512]{1,0:T(8,128)S(1)} %fusion.1), channel_id=1, source_target_pairs={{0,4},{4,0},{8,12},{12,8},{1,5},{5,1},{9,13},{13,9},{2,6},{6,2},{1... | collective-permute-start | bytes 393224 | tf_op jit(solution)/shard_map/ppermute | solution.py:18
  137.1 4.8 %collective-permute-start.9 = (bf16[64,1024]{1,0:T(8,128)(2,1)S(1)}, bf16[64,1024]{1,0:T(8,128)(2,1)S(1)}, u32[]{:S(2)}, u32[]{:S(2)}) collective-permute-start(bf16[64,1024]{1,0:T(8,128)(2,1)S(1)} %collective-permute-done.8), channel_id=1, source_target_pairs={{0,1},{1,0},{2,3},{3,2},{4,5},{5,4},{6,7},{7,6},{8,9},{9,8},{10,11... | collective-permute-start | bytes 393224 | tf_op jit(solution)/shard_map/ppermute | solution.py:18
  137.3 4.5 %copy-start.13 = (bf16[64,1024]{1,0:T(8,128)(2,1)S(1)}, bf16[64,1024]{1,0:T(8,128)(2,1)}, u32[]{:S(2)}) copy-start(bf16[64,1024]{1,0:T(8,128)(2,1)} %copy-done.12) | copy-start | bytes 393220
  141.9 8.5 %collective-permute-start.1 = (f32[64,512]{1,0:T(8,128)S(1)}, f32[64,512]{1,0:T(8,128)S(1)}, u32[]{:S(2)}, u32[]{:S(2)}) collective-permute-start(f32[64,512]{1,0:T(8,128)S(1)} %add.24), channel_id=1, source_target_pairs={{0,8},{4,12},{8,0},{12,4},{1,9},{5,13},{9,1},{13,5},{2,10},{6,14},... | collective-permute-start | bytes 393224 | tf_op jit(solution)/shard_map/ppermute | solution.py:18
  150.4 101.0 %collective-permute-start.15 = (bf16[512,1024]{1,0:T(8,128)(2,1)}, bf16[512,1024]{1,0:T(8,128)(2,1)S(1)}, u32[]{:S(2)}, u32[]{:S(2)}) collective-permute-start(bf16[512,1024]{1,0:T(8,128)(2,1)} %get-tuple-element.15), channel_id=1, source_target_pairs={{0,2},{1,3},{2,0},{3,1},{4,6},{5,7},{6,4},{7,5},{8,10},{9,11},{10,... | collective-permute-start | bytes 3145736 | tf_op jit(solution)/shard_map/ppermute | solution.py:18
  154.0 110.9 %collective-permute-start.14 = (bf16[512,512]{1,0:T(8,128)(2,1)}, bf16[512,512]{1,0:T(8,128)(2,1)S(1)}, u32[]{:S(2)}, u32[]{:S(2)}) collective-permute-start(bf16[512,512]{1,0:T(8,128)(2,1)} %slice.14), channel_id=1, source_target_pairs={{0,2},{1,3},{2,0},{3,1},{4,6},{5,7},{6,4},{7,5},{8,10},{9,11},{10,... | collective-permute-start | bytes 1572872 | tf_op jit(solution)/shard_map/ppermute | solution.py:18
  154.7 52.0 %collective-permute-start.13 = (bf16[2,512,512]{2,1,0:T(8,128)(2,1)}, bf16[2,512,512]{2,1,0:T(8,128)(2,1)S(1)}, u32[]{:S(2)}, u32[]{:S(2)}) collective-permute-start(bf16[2,512,512]{2,1,0:T(8,128)(2,1)} %collective-permute-done.12.refs_2_), channel_id=1, source_target_pairs={{0,4},{4,8},{8,12},{12,0},{1,5},{5,9},{9,13},{13,1},{2,6},{6,10},{... | collective-permute-start | bytes 3145736 | tf_op jit(solution)/shard_map/ppermute | solution.py:210
  206.8 1.0 copy-start.3
  251.5 1.0 copy-start.6
  264.8 14.7 %copy-start.5 = (f32[64,512]{1,0:T(8,128)S(1)}, f32[64,512]{1,0:T(8,128)}, u32[]{:S(2)}) copy-start(f32[64,512]{1,0:T(8,128)} %project.7.refs_8_) | copy-start | bytes 393220
  264.9 0.8 copy-start.7
  265.7 30.3 %copy-start.1 = (bf16[512,2048]{1,0:T(8,128)(2,1)S(1)}, bf16[512,2048]{1,0:T(8,128)(2,1)}, u32[]{:S(2)}) copy-start(bf16[512,2048]{1,0:T(8,128)(2,1)} %param.7) | copy-start | bytes 6291460
  274.3 5.2 %collective-permute-start.17 = (f32[64,512]{1,0:T(8,128)}, f32[64,512]{1,0:T(8,128)S(1)}, u32[]{:S(2)}, u32[]{:S(2)}) collective-permute-start(f32[64,512]{1,0:T(8,128)} %project.11), channel_id=1, source_target_pairs={{0,2},{1,3},{2,0},{3,1},{4,6},{5,7},{6,4},{7,5},{8,10},{9,11},{10,... | collective-permute-start | bytes 393224 | tf_op jit(solution)/shard_map/ppermute | solution.py:18
  279.6 5.0 %collective-permute-start.18 = (f32[64,512]{1,0:T(8,128)S(1)}, f32[64,512]{1,0:T(8,128)S(1)}, u32[]{:S(2)}, u32[]{:S(2)}) collective-permute-start(f32[64,512]{1,0:T(8,128)S(1)} %add.30), channel_id=1, source_target_pairs={{0,4},{4,0},{8,12},{12,8},{1,5},{5,1},{9,13},{13,9},{2,6},{6,2},{1... | collective-permute-start | bytes 393224 | tf_op jit(solution)/shard_map/ppermute | solution.py:18
  284.6 7.3 %copy-start.8 = (f32[64,512]{1,0:T(8,128)}, f32[64,512]{1,0:T(8,128)S(1)}, u32[]{:S(2)}) copy-start(f32[64,512]{1,0:T(8,128)S(1)} %add.31.grad_ref) | copy-start | bytes 393220
  284.6 7.3 %collective-permute-start.19 = (f32[64,512]{1,0:T(8,128)S(1)}, f32[64,512]{1,0:T(8,128)S(1)}, u32[]{:S(2)}, u32[]{:S(2)}) collective-permute-start(f32[64,512]{1,0:T(8,128)S(1)} %add.31.grad_ref), channel_id=1, source_target_pairs={{0,8},{4,12},{8,0},{12,4},{1,9},{5,13},{9,1},{13,5},{2,10},{6,14},... | collective-permute-start | bytes 393224 | tf_op jit(solution)/shard_map/ppermute | solution.py:18
  292.0 0.7 copy-start.10
